TPU v7x, 512 devices: a whole 4x8x8 slice. The times are simulated.
512 devices in a mesh: req: 8 (over x, core), pre: 64 (over y, z).
Axes of the slice: x: 4, y: 8, z: 8, core: 2. Of those that a mesh axis runs over, the one named last changes fastest.
Arguments:
- queries: bfloat16 [4, 64, 8192], P(None, 'req', 'pre')
- prefix_cache: bfloat16 [2, 32768, 1024], P(None, 'pre')
- suffix_pool: bfloat16 [2, 16384, 16, 1024], P(None, ('req', 'pre')), may hold values from -6 to 6
- suffix_lengths: int32 [64], P('req'), may hold values from 1 to 4092, 131072 in all
- page_table: int32 [64, 256], P('req'), may hold values from 0 to 16383, as said below
- out_weight: bfloat16 [8192, 8192], P('pre', 'req'), may hold values from -0.0625 to 0.0625
Outputs:
- attended: float32 [4, 64, 8192], P(None, 'req', 'pre')
- projected: float32 [256, 8192], P('pre', 'req')
Inputs may be any that keep to these rules, and one draw needn't show every extreme that they name: Cached suffix tokens before the first new position; the keys of the 4 new positions sit at suffix tokens suffix_lengths[r] onward; some request has exactly 4092. `page_table`: the requests of aligned block b of 8 requests together hold each pool page b * 8 * 256 to (b + 1) * 8 * 256 - 1 exactly once.
All inputs are finite; a program needn't handle non-finite values. No bound on the sum of `suffix_lengths` on one device may be relied on, other than what follows from the above.
Results may differ from a plain program's by a relative error of at most 0.0075.
Values may be sent and summed in bfloat16 or wider, within the bound.
No kernel may reach another device: no remote copies, remote signals or barrier semaphores. Data moves between devices by JAX's collectives and lax.ppermute only.
A program may use at most 64 MiB of HBM per device.

v0:
```python
import math

import jax
import jax.numpy as jnp
from jax import lax
from jax.sharding import PartitionSpec as P

H = 64
KVH = 8
HD = 128


def body(queries, prefix_cache, suffix_pool, suffix_lengths, page_table, out_weight):
    step_count = queries.shape[0]
    local_requests = queries.shape[1]
    per_group = H // KVH
    gathered = lax.all_gather(queries, "pre", axis=2, tiled=True)
    query_tiles = gathered.reshape(step_count, local_requests, KVH, per_group, HD)
    slot_count = suffix_pool.shape[1]
    page_length = suffix_pool.shape[2]
    suffix_tokens = slot_count * page_length
    prefix_tokens = prefix_cache.shape[1]
    all_keys = jnp.concatenate(
        [prefix_cache[0], suffix_pool[0].reshape(suffix_tokens, KVH * HD)], 0
    )
    all_keys = all_keys.reshape(prefix_tokens + suffix_tokens, KVH, HD)
    all_values = jnp.concatenate(
        [prefix_cache[1], suffix_pool[1].reshape(suffix_tokens, KVH * HD)], 0
    )
    all_values = all_values.reshape(prefix_tokens + suffix_tokens, KVH, HD)
    scores = jnp.einsum(
        "srgxd,tgd->srgxt", query_tiles, all_keys, preferred_element_type=jnp.float32
    )
    scores = scores * (1.0 / math.sqrt(HD))
    first_slot = (lax.axis_index("req") * lax.axis_size("pre") + lax.axis_index("pre")) * slot_count
    slot_ids = first_slot + jnp.arange(slot_count, dtype=jnp.int32)
    matches = page_table[:, :, None] == slot_ids[None, None, :]
    owned = jnp.any(matches, axis=1)
    page_rank = jnp.arange(page_table.shape[1], dtype=jnp.int32)
    page_number = jnp.sum(jnp.where(matches, page_rank[None, :, None], 0), axis=(0, 1))
    offsets = jnp.arange(page_length, dtype=jnp.int32)
    positions = (page_number[:, None] * page_length + offsets[None, :]).reshape(suffix_tokens)
    owned_tokens = jnp.repeat(owned, page_length, axis=1)
    limits = suffix_lengths[None, :] + jnp.arange(step_count, dtype=jnp.int32)[:, None] + 1
    seen = owned_tokens[None, :, :] & (positions[None, None, :] < limits[:, :, None])
    prefix_seen = jnp.ones((step_count, local_requests, prefix_tokens), dtype=bool)
    visible = jnp.concatenate([prefix_seen, seen], 2)[:, :, None, None, :]
    scores = jnp.where(visible, scores, -jnp.inf)
    row_max = jnp.max(scores, axis=-1)
    exps = jnp.exp(scores - row_max[..., None])
    weight_sum = jnp.sum(exps, axis=-1)
    weights = exps.astype(jnp.bfloat16)
    numerator = jnp.einsum(
        "srgxt,tgd->srgxd", weights, all_values, preferred_element_type=jnp.float32
    )
    numerator = numerator.reshape(step_count, local_requests, H * HD)
    row_max = row_max.reshape(step_count, local_requests, H)
    weight_sum = weight_sum.reshape(step_count, local_requests, H)
    peak = lax.pmax(row_max, "pre")
    factor = jnp.exp(row_max - peak)
    scaled = numerator * jnp.repeat(factor, HD, axis=2)
    summed, totals = (
        lax.psum_scatter(scaled, "pre", scatter_dimension=2, tiled=True),
        lax.psum_scatter(weight_sum * factor, "pre", scatter_dimension=2, tiled=True),
    )
    attended = summed / jnp.repeat(totals, HD, axis=2)
    rounded = jnp.transpose(attended.astype(jnp.bfloat16), (1, 0, 2))
    every_request = lax.all_gather(rounded, "req", axis=0, tiled=True)
    flat_rows = every_request.reshape(every_request.shape[0] * step_count, every_request.shape[2])
    projected = lax.psum_scatter(
        jnp.dot(flat_rows, out_weight, preferred_element_type=jnp.float32),
        "pre",
        scatter_dimension=0,
        tiled=True,
    )
    return (attended, projected)


def solution(mesh):
    placed = (
        P(None, "req", "pre"),
        P(None, "pre", None),
        P(None, ("req", "pre"), None, None),
        P("req"),
        P("req", None),
        P("pre", "req"),
    )
    return jax.shard_map(
        body,
        mesh=mesh,
        in_specs=placed,
        out_specs=(P(None, "req", "pre"), P("pre", "req")),
        check_vma=False,
    )
```

profile of v0, /device:TPU:2, one launch (start us, length us, event | category | flops | bytes accessed | tf_op | source)
XLA Modules:
  0.0 819.4 jit_solution(14686681188668805055)
XLA Ops:
  7.2 1.0 compare_reduce_fusion
  8.3 0.9 fusion.18
  9.6 1.2 add_add_fusion
  10.8 1.7 fusion.24
  12.6 0.5 copy.61
  13.1 0.7 copy.49
  13.8 1.7 fusion.25
  15.9 57.6 %all_gather.6 = bf16[4,8,8192]{2,1,0:T(8,128)(2,1)S(1)} all-gather(bf16[4,8,128]{2,1,0:T(8,128)(2,1)S(1)} %copy-done.4), channel_id=1, replica_groups=mesh['req'=8,'pre'=64] {'pre'}, dimensions={2}, use_global_device_ids=true | all-gather | bytes 532480 | tf_op jit(solution)/shard_map/all_gather | solution.py:17
  73.6 1.7 fusion.2
  75.4 3.1 copy-done.1
  78.5 2.4 fusion
  81.2 276.6 %pmax.7 = f32[4,8,64]{2,1,0:T(8,128)S(1)} all-reduce(f32[4,8,64]{2,1,0:T(8,128)S(1)} %reshape.83), channel_id=1, replica_groups=mesh['req'=8,'pre'=64] {'pre'}, use_global_device_ids=true, to_apply=%region_3.4 | all-reduce | flops 2048 | bytes 16384 | tf_op jit(solution)/shard_map/pmax | solution.py:59
  357.8 0.8 copy.54
  359.1 0.7 copy.46
  360.2 4.7 fusion.14
  365.2 1.3 bitcast_multiply_fusion
  366.8 1.3 dynamic-slice
  368.0 274.0 %all-reduce.1 = f32[4,8,64]{1,0,2:T(4,128)S(1)} all-reduce(f32[4,8,64]{1,0,2:T(4,128)S(1)} %copy.56), channel_id=3, replica_groups=mesh['req'=8,'pre'=64] {'pre'}, use_global_device_ids=true, to_apply=%region_6.7.clone | all-reduce | flops 2048 | bytes 16384
  642.1 0.6 dynamic-slice_bitcast_fusion
  642.8 1.4 convert_bitcast_fusion
  644.2 11.5 %all_gather.7 = bf16[64,4,128]{2,0,1:T(8,128)(2,1)S(1)} all-gather(bf16[8,4,128]{2,0,1:T(8,128)(2,1)S(1)} %get-tuple-element.2), channel_id=1, replica_groups=mesh['req'=8,'pre'=64] {'req'}, dimensions={0}, use_global_device_ids=true | all-gather | bytes 73728 | tf_op jit(solution)/shard_map/all_gather | solution.py:68
  655.8 1.3 fusion.26
  657.8 153.5 %all-reduce.5.cloned.1.call-done = f32[256,1024]{1,0:T(8,128)} async-done(((f32[256,1024]{1,0:T(8,128)}), f32[256,1024]{1,0:T(8,128)}) %all-reduce.5.cloned.1.call-update) | async-done | bytes 1048592
  811.2 1.4 constant_dynamic-slice_fusion
  (38 shorter events, 2.8 us)
Async XLA Ops:
  7.2 648.6 %copy-start = (bf16[128,1024]{1,0:T(8,128)(2,1)S(1)}, bf16[128,1024]{1,0:T(8,128)(2,1)}, u32[]{:S(2)}) copy-start(bf16[128,1024]{1,0:T(8,128)(2,1)} %param.11) | copy-start | bytes 786436
  7.2 635.6 %reduce-scatter.2.cloned.1.call-start = ((), (), s32[]{:S(2)}) async-start(), calls=%async_computation.1 | async-start | bytes 1064960 | tf_op jit(solution)/shard_map/reduce_scatter | solution.py:63
  10.8 5.1 copy-start.4
  13.1 60.4 %copy-start.5 = (s32[4,8]{1,0:T(4,128)S(1)}, s32[4,8]{1,0:T(4,128)}, u32[]{:S(2)}) copy-start(s32[4,8]{1,0:T(4,128)} %add_add_fusion) | copy-start | bytes 388
  73.6 7.3 copy-start.3
  75.3 3.2 copy-start.1
  360.2 5.1 copy-start.2
  366.6 444.6 %all-reduce.5.cloned.1.call-start = ((), (), s32[]{:S(2)}) async-start(), calls=%async_computation.2 | async-start | bytes 2097152
Sparse Core Ops, SparseCore 0:
  366.7 238.2 reduce-scatter.1
  657.2 153.9 all-reduce.4
where the time goes:
time: 820 us; the launch traced here: 819 us
  blocking collectives  620 us (76%)
  waiting for transfers between devices  154 us (19%)
  local copies, waits for them, and re-layouts  15 us (2%)
  between operations  15 us (2%)
  other arithmetic  8.43 us (1%)
    pmax x1, blocking collectives, body(): peak = lax.pmax(row_max, 'pre')  277 us
    unnamed x1, blocking collectives  274 us
    unnamed x3, waiting for transfers between devices  154 us
    all_gather x1, blocking collectives, body(): gathered = lax.all_gather(queries, 'pre', axis=2, tiled=True)  57.6 us
  transfers between devices with their start and end apart: 2, of which 1 were waited for; matrix products, arithmetic and copies ran while one was open for 0% of the time, Pallas kernels for 0%

commit v1 on v0

v1 whole, which is shorter than its diff:
```python
import math

import jax
import jax.numpy as jnp
from jax import lax
from jax.sharding import PartitionSpec as P

H = 64
KVH = 8
HD = 128


def exchange(blocks, axis):
    return lax.all_to_all(blocks, axis, 0, 0, tiled=True)


def body(queries, prefix_cache, suffix_pool, suffix_lengths, page_table, out_weight):
    step_count, local_requests, _ = queries.shape
    rows = step_count * local_requests
    per_group = H // KVH
    holders = lax.axis_size("pre")
    members = lax.axis_size("req")
    own = jnp.transpose(queries, (1, 0, 2)).reshape(1, rows, HD)
    gathered = exchange(jnp.broadcast_to(own, (holders, rows, HD)), "pre")
    query_tiles = gathered.reshape(KVH, per_group * rows, HD)

    slot_count = suffix_pool.shape[1]
    page_length = suffix_pool.shape[2]
    suffix_tokens = slot_count * page_length
    prefix_tokens = prefix_cache.shape[1]
    first_slot = (lax.axis_index("req") * holders + lax.axis_index("pre")) * slot_count
    slot_ids = first_slot + jnp.arange(slot_count, dtype=jnp.int32)
    matches = page_table[:, :, None] == slot_ids[None, None, :]
    owned = jnp.any(matches, axis=1)
    page_rank = jnp.arange(page_table.shape[1], dtype=jnp.int32)
    page_number = jnp.sum(jnp.where(matches, page_rank[None, :, None], 0), axis=(0, 1))
    offsets = jnp.arange(page_length, dtype=jnp.int32)
    positions = (page_number[:, None] * page_length + offsets[None, :]).reshape(suffix_tokens)
    owned_tokens = jnp.repeat(owned, page_length, axis=1)
    limits = suffix_lengths[:, None] + jnp.arange(step_count, dtype=jnp.int32)[None, :] + 1
    seen = owned_tokens[:, None, :] & (positions[None, None, :] < limits[:, :, None])
    seen = seen.reshape(1, 1, rows, suffix_tokens)

    scale = 1.0 / math.sqrt(HD)

    def score(keys):
        tiles = keys.reshape(-1, KVH, HD)
        return scale * jnp.einsum("gmd,tgd->gmt", query_tiles, tiles, preferred_element_type=jnp.float32)

    prefix_scores = score(prefix_cache[0])
    suffix_scores = score(suffix_pool[0]).reshape(KVH, per_group, rows, suffix_tokens)
    suffix_scores = jnp.where(seen, suffix_scores, -jnp.inf).reshape(KVH, per_group * rows, suffix_tokens)
    row_max = jnp.maximum(jnp.max(prefix_scores, axis=-1), jnp.max(suffix_scores, axis=-1))
    prefix_exps = jnp.exp(prefix_scores - row_max[..., None])
    suffix_exps = jnp.exp(suffix_scores - row_max[..., None])
    weight_sum = jnp.sum(prefix_exps, axis=-1) + jnp.sum(suffix_exps, axis=-1)

    def weigh(exps, values):
        tiles = values.reshape(-1, KVH, HD)
        return jnp.einsum(
            "gmt,tgd->gmd", exps.astype(jnp.bfloat16), tiles, preferred_element_type=jnp.float32
        )

    numerator = weigh(prefix_exps, prefix_cache[1]) + weigh(suffix_exps, suffix_pool[1])
    share = (numerator / weight_sum[..., None]).astype(jnp.bfloat16).reshape(holders, rows, HD)
    log_total = (row_max + jnp.log(weight_sum)).reshape(holders, rows)
    high = lax.reduce_precision(log_total, 8, 7)
    rest = log_total - high
    middle = lax.reduce_precision(rest, 8, 7)
    stats = jnp.stack([high, middle, rest - middle], 1).astype(jnp.bfloat16)
    stats = jnp.pad(stats, ((0, 0), (0, 5), (0, HD - rows)))
    received = exchange(jnp.concatenate([share, stats], 1), "pre")
    shares = received[:, :rows].astype(jnp.float32)
    parts = received[:, rows : rows + 3, :rows].astype(jnp.float32)
    logs = parts[:, 0] + parts[:, 1] + parts[:, 2]
    factor = jnp.exp(logs - jnp.max(logs, axis=0))
    merged = jnp.sum(shares * factor[..., None], axis=0) / jnp.sum(factor, axis=0)[:, None]
    attended = jnp.transpose(merged.reshape(local_requests, step_count, HD), (1, 0, 2))

    rounded = merged.astype(jnp.bfloat16)
    flat_rows = exchange(jnp.broadcast_to(rounded[None], (members, rows, HD)), "req")
    flat_rows = flat_rows.reshape(members * rows, HD)
    partial = jnp.dot(flat_rows, out_weight, preferred_element_type=jnp.float32)
    columns = out_weight.shape[1] // HD
    blocks = partial.astype(jnp.bfloat16).reshape(holders, step_count, columns, HD)
    blocks = jnp.transpose(blocks, (0, 2, 1, 3)).reshape(holders, columns * step_count, HD)
    pieces = exchange(blocks, "pre")
    projected = jnp.sum(pieces.astype(jnp.float32), axis=0).reshape(columns, step_count, HD)
    projected = jnp.transpose(projected, (1, 0, 2)).reshape(step_count, columns * HD)
    return (attended, projected)


def solution(mesh):
    placed = (
        P(None, "req", "pre"),
        P(None, "pre", None),
        P(None, ("req", "pre"), None, None),
        P("req"),
        P("req", None),
        P("pre", "req"),
    )
    return jax.shard_map(
        body,
        mesh=mesh,
        in_specs=placed,
        out_specs=(P(None, "req", "pre"), P("pre", "req")),
        check_vma=False,
    )
```

time: 820 us -> 113 us (0.14)
  the two profiles are of different devices: /device:TPU:2 before, /device:TPU:16 now
where the time goes in v1:
time: 113 us; the launch traced here: 112 us
  blocking collectives  36.4 us (32%)
  waiting for transfers between devices  27.7 us (25%)
  starting transfers between devices  21.8 us (19%)
  local copies, waits for them, and re-layouts  12.2 us (11%)
  matrix products  6.7 us (6%)
  other arithmetic  6.44 us (6%)
    all_to_all x2, blocking collectives, exchange(): return lax.all_to_all(blocks, axis, 0, 0, tiled=True)  36.4 us
    all_to_all x2, waiting for transfers between devices, exchange(): return lax.all_to_all(blocks, axis, 0, 0, tiled=True)  27.7 us
    all_to_all x2, starting transfers between devices, exchange(): return lax.all_to_all(blocks, axis, 0, 0, tiled=True)  21.8 us
    unnamed x15, local copies, waits for them, and re-layouts  5.18 us
    dot_general x2, matrix products, weigh(): jnp.einsum('gmt,tgd->gmd', exps.astype(jnp.bfloat16), tiles, preferred_el...  4.7 us
  transfers between devices with their start and end apart: 2, of which 2 were waited for; matrix products, arithmetic and copies ran while one was open for 10% of the time, Pallas kernels for 0%

profile of v1, /device:TPU:16, one launch (start us, length us, event | category | flops | bytes accessed | tf_op | source)
XLA Modules:
  0.0 112.2 jit_solution(6419371596000632349)
XLA Ops:
  0.6 0.7 copy.32
  1.4 0.9 broadcast_in_dim.37
  2.2 16.5 %all-to-all-start = ((bf16[64,32,128]{2,1,0:T(8,128)(2,1)}), bf16[64,32,128]{2,1,0:T(8,128)(2,1)S(1)}, u32[]{:S(2)}, u32[]{:S(2)}) async-start(bf16[64,32,128]{2,1,0:T(8,128)(2,1)} %broadcast_in_dim.37), calls=%async_computation | async-start | bytes 1048576 | tf_op jit(solution)/shard_map/all_to_all | solution.py:14
  18.7 0.9 fusion.26
  19.7 0.7 add_add_fusion
  20.6 1.0 compare_reduce_fusion
  21.9 1.7 %fusion.33 = (bf16[1,512,1024]{2,1,0:T(8,128)(2,1)S(1)}, bf16[1,512,1024]{2,1,0:T(8,128)(2,1)S(1)}) fusion(bf16[2,512,1024]{2,1,0:T(8,128)(2,1)} %param.7), kind=kLoop, calls=%fused_computation.55 | loop fusion | bytes 4194304 | tf_op jit(solution)/shard_map/slice | solution.py:64
  23.6 1.3 %copy.46 = bf16[1,512,1024]{1,2,0:T(8,128)(2,1)} copy(bf16[1,512,1024]{2,1,0:T(8,128)(2,1)S(1)} %get-tuple-element.16) | data formatting | bytes 2097152
  25.5 1.7 %fusion.34 = (bf16[1,32,16,1024]{3,2,1,0:T(8,128)(2,1)S(1)}, bf16[1,32,16,1024]{3,2,1,0:T(8,128)(2,1)S(1)}) fusion(bf16[2,32,16,1024]{3,2,1,0:T(8,128)(2,1)} %param.8), kind=kLoop, calls=%fused_computation.56 | loop fusion | bytes 4194304 | tf_op jit(solution)/shard_map/slice | solution.py:64
  27.2 1.3 %copy.49 = bf16[64,8,8,128]{3,2,1,0:T(8,128)(2,1)} copy(bf16[64,8,8,128]{3,1,2,0:T(8,128)(2,1)S(1)} %bitcast.43) | data formatting | bytes 2097152
  28.9 9.2 %all-to-all-done = bf16[64,32,128]{2,1,0:T(8,128)(2,1)S(1)} async-done(((bf16[64,32,128]{2,1,0:T(8,128)(2,1)}), bf16[64,32,128]{2,1,0:T(8,128)(2,1)S(1)}, u32[]{:S(2)}, u32[]{:S(2)}) %all-to-all-start) | async-done | bytes 524320 | tf_op jit(solution)/shard_map/all_to_all | solution.py:14
  38.1 0.8 multiply_reduce_fusion
  39.0 1.0 fusion
  39.9 1.0 copy-done.3
  40.9 1.4 %fusion.5 = f32[8,256,128]{2,1,0:T(8,128)S(1)} fusion(f32[8,256,512]{2,1,0:T(8,128)S(1)} %get-tuple-element.26, f32[8,256]{1,0:T(8,128)S(1)} %max.24, pred[256,512]{1,0:T(8,128)(4,1)S(1)} %bitcast.47, bf16[512,8,128]{2,1,0:T(8,128)(2,1)S(1)} %bitcast.50), kind=kOutput, calls=%fused_computation.9 | convolution fusion | flops 272629760 | bytes 6430720 | tf_op jit(solution)/shard_map/gmt,tgd->gmd/dot_general | solution.py:60
  42.3 2.2 %fusion.3 = (f32[8,256]{1,0:T(8,128)S(1)}, f32[8,256]{1,0:T(8,128)S(1)}) fusion(f32[8,256,512]{2,1,0:T(8,128)S(1)} %get-tuple-element.26, f32[8,256]{1,0:T(8,128)S(1)} %max.24, pred[256,512]{1,0:T(8,128)(4,1)S(1)} %bitcast.48, f32[8,256,512]{2,1,0:T(8,128)S(1)} %get-tuple-element.24), kind=kLoop, calls=%fused_computation.7 | loop fusion | flops 7335936 | bytes 8544256 | tf_op jit(solution)/shard_map/reduce_sum | solution.py:56
  44.7 3.3 %divide_convert_fusion = bf16[8,256,128]{2,1,0:T(8,128)(2,1)S(1)} fusion(f32[8,256,128]{2,1,0:T(8,128)S(1)} %fusion.5, bf16[512,8,128]{0,2,1:T(8,128)(2,1)S(1)} %bitcast.49, f32[8,256,512]{2,1,0:T(8,128)} %copy-done.1, f32[8,256]{1,0:T(8,128)S(1)} %max.24, f32[8,256]{1,0:T(8,128)S(1)} %get-tuple-element.15), kind=kOutput, calls=%fused_computation.27 | convolution fusion | flops 272367616 | bytes 6832128 | tf_op jit(solution)/shard_map/gmt,tgd->gmd/dot_general | solution.py:60
  48.1 26.7 %all_to_all.20 = bf16[64,40,128]{2,1,0:T(8,128)(2,1)S(1)} all-to-all(bf16[64,40,128]{2,1,0:T(8,128)(2,1)S(1)} %fusion.25), channel_id=1, replica_groups=mesh['req'=8,'pre'=64] {'pre'}, dimensions={0} | all-to-all | bytes 1310720 | tf_op jit(solution)/shard_map/all_to_all | solution.py:14
  75.4 9.7 %all_to_all.21 = bf16[8,32,128]{2,1,0:T(8,128)(2,1)S(1)} all-to-all(bf16[8,32,128]{2,1,0:T(8,128)(2,1)S(1)} %broadcast_in_dim.67), channel_id=1, replica_groups=mesh['req'=8,'pre'=64] {'req'}, dimensions={0} | all-to-all | bytes 131072 | tf_op jit(solution)/shard_map/all_to_all | solution.py:14
  85.7 1.1 %copy.41 = bf16[64,32,128]{2,1,0:T(8,128)(2,1)} copy(bf16[64,32,128]{2,0,1:T(8,128)(2,1)S(1)} %bitcast.45) | data formatting | bytes 1048576 | tf_op jit(solution)/shard_map/reshape | solution.py:86
  86.9 5.3 %all-to-all-start.3 = ((bf16[64,32,128]{2,1,0:T(8,128)(2,1)}), bf16[64,32,128]{2,1,0:T(8,128)(2,1)S(1)}, u32[]{:S(2)}, u32[]{:S(2)}) async-start(bf16[64,32,128]{2,1,0:T(8,128)(2,1)} %copy.41), calls=%async_computation.3 | async-start | bytes 1048576 | tf_op jit(solution)/shard_map/all_to_all | solution.py:14
  92.4 0.6 copy.42
  93.0 18.5 %all-to-all-done.3 = bf16[64,32,128]{2,1,0:T(8,128)(2,1)S(1)} async-done(((bf16[64,32,128]{2,1,0:T(8,128)(2,1)}), bf16[64,32,128]{2,1,0:T(8,128)(2,1)S(1)}, u32[]{:S(2)}, u32[]{:S(2)}) %all-to-all-start.3) | async-done | bytes 524320 | tf_op jit(solution)/shard_map/all_to_all | solution.py:14
  111.5 0.7 convert_reduce_fusion
  (38 shorter events, 3.0 us)
Async XLA Ops:
  0.6 84.5 %copy-start = (bf16[128,1024]{1,0:T(8,128)(2,1)S(1)}, bf16[128,1024]{1,0:T(8,128)(2,1)}, u32[]{:S(2)}) copy-start(bf16[128,1024]{1,0:T(8,128)(2,1)} %param.11) | copy-start | bytes 786436
  2.2 35.9 %all-to-all-start = ((bf16[64,32,128]{2,1,0:T(8,128)(2,1)}), bf16[64,32,128]{2,1,0:T(8,128)(2,1)S(1)}, u32[]{:S(2)}, u32[]{:S(2)}) async-start(bf16[64,32,128]{2,1,0:T(8,128)(2,1)} %broadcast_in_dim.37), calls=%async_computation | async-start | bytes 1048576 | tf_op jit(solution)/shard_map/all_to_all | solution.py:14
  38.9 3.4 %copy-start.1 = (f32[8,256,512]{2,1,0:T(8,128)}, f32[8,256,512]{2,1,0:T(8,128)S(1)}, u32[]{:S(2)}) copy-start(f32[8,256,512]{2,1,0:T(8,128)S(1)} %get-tuple-element.24) | copy-start | bytes 12582916
  38.9 2.0 %copy-start.3 = (bf16[64,8,8,128]{3,2,1,0:T(8,128)(2,1)S(1)}, bf16[64,8,8,128]{3,2,1,0:T(8,128)(2,1)}, u32[]{:S(2)}) copy-start(bf16[64,8,8,128]{3,2,1,0:T(8,128)(2,1)} %copy.49) | copy-start | bytes 3145732
  42.3 2.4 %copy-start.2 = (bf16[1,512,1024]{1,2,0:T(8,128)(2,1)S(1)}, bf16[1,512,1024]{1,2,0:T(8,128)(2,1)}, u32[]{:S(2)}) copy-start(bf16[1,512,1024]{1,2,0:T(8,128)(2,1)} %copy.46) | copy-start | bytes 3145732
  86.9 24.6 %all-to-all-start.3 = ((bf16[64,32,128]{2,1,0:T(8,128)(2,1)}), bf16[64,32,128]{2,1,0:T(8,128)(2,1)S(1)}, u32[]{:S(2)}, u32[]{:S(2)}) async-start(bf16[64,32,128]{2,1,0:T(8,128)(2,1)} %copy.41), calls=%async_computation.3 | async-start | bytes 1048576 | tf_op jit(solution)/shard_map/all_to_all | solution.py:14

commit v2 on v1

v2 whole, which is shorter than its diff:
```python
import math

import jax
import jax.numpy as jnp
from jax import lax
from jax.experimental import pallas as pl
from jax.experimental.pallas import tpu as pltpu
from jax.sharding import PartitionSpec as P

H = 64
KVH = 8
HD = 128
STAT_ROWS = 8
PRE = "pre"
MEGA = 1024 * 1024


def exchange(blocks, axis):
    return lax.all_to_all(blocks, axis, 0, 0, tiled=True)


def in_hbm(array):
    return pltpu.with_memory_space_constraint(array, pltpu.HBM)


def in_vmem(array):
    return pltpu.with_memory_space_constraint(array, pltpu.VMEM)


def spread_kernel(own_ref, out_ref):
    step_count, local_requests, _ = own_ref.shape
    own = own_ref[...].astype(jnp.float32)
    ordered = jnp.concatenate(
        [
            own[step, request : request + 1]
            for request in range(local_requests)
            for step in range(step_count)
        ],
        0,
    ).astype(out_ref.dtype)
    for holder in range(out_ref.shape[0]):
        out_ref[holder] = ordered


def spread(own, holders):
    rows = own.shape[0] * own.shape[1]
    return pl.pallas_call(
        spread_kernel,
        out_specs=pl.BlockSpec(memory_space=pltpu.VMEM),
        out_shape=pltpu.VMEM((holders, rows, HD), own.dtype),
        name="spread",
        compiler_params=pltpu.CompilerParams(vmem_limit_bytes=4 * MEGA),
    )(in_hbm(own))


def stage_kernel(prefix_ref, suffix_ref, keys_ref, sems):
    copies = [
        pltpu.make_async_copy(prefix_ref.at[0], keys_ref.at[0], sems.at[0]),
        pltpu.make_async_copy(suffix_ref.at[0], keys_ref.at[1], sems.at[1]),
    ]
    for copy in copies:
        copy.start()
    for copy in copies:
        copy.wait()


def stage(prefix_cache, suffix_cache):
    return pl.pallas_call(
        stage_kernel,
        in_specs=[pl.BlockSpec(memory_space=pl.ANY)] * 2,
        out_specs=pl.BlockSpec(memory_space=pltpu.VMEM),
        out_shape=pltpu.VMEM(prefix_cache.shape, prefix_cache.dtype),
        scratch_shapes=[pltpu.SemaphoreType.DMA((2,))],
        name="stage",
        compiler_params=pltpu.CompilerParams(vmem_limit_bytes=4 * MEGA),
        cost_estimate=pl.CostEstimate(flops=0, bytes_accessed=4 * MEGA, transcendentals=0),
    )(in_hbm(prefix_cache), in_hbm(suffix_cache))


def split(value):
    high = value.astype(jnp.bfloat16).astype(jnp.float32)
    rest = value - high
    middle = rest.astype(jnp.bfloat16).astype(jnp.float32)
    return high, middle, rest - middle


def attend_kernel(query_ref, keys_ref, prefix_hbm, suffix_hbm, mask_ref, out_ref, values_ref, sems):
    rows = query_ref.shape[1]
    per_group = H // KVH
    width = per_group * rows
    line = lax.broadcasted_iota(jnp.int32, (STAT_ROWS, width), 0)
    factor = math.log2(math.e) / math.sqrt(HD)
    suffix_tokens = mask_ref.shape[1]

    def lanes(group):
        return slice(group * HD, (group + 1) * HD)

    copies = []
    for group in range(KVH):
        part = pl.ds(group * HD, HD)
        for half, cache in enumerate((prefix_hbm, suffix_hbm)):
            copy = pltpu.make_async_copy(
                cache.at[1, :, part], values_ref.at[half, :, part], sems.at[half, group]
            )
            copy.start()
            copies.append(copy)

    def scores(group):
        query = query_ref[group * per_group : (group + 1) * per_group].reshape(width, HD)

        def score(keys):
            return lax.dot_general(query, keys, (((1,), (1,)), ((), ())), preferred_element_type=jnp.float32)

        prefix_scores = score(keys_ref[0, :, lanes(group)])
        suffix_scores = score(keys_ref[1, :, lanes(group)]).reshape(per_group, rows, suffix_tokens)
        return prefix_scores, (suffix_scores + mask_ref[...][None]).reshape(width, suffix_tokens)

    def weigh(group, prefix_scores, suffix_scores):
        row_max = jnp.maximum(
            jnp.max(prefix_scores, axis=1, keepdims=True), jnp.max(suffix_scores, axis=1, keepdims=True)
        )
        shift = row_max * factor
        prefix_exps = jnp.exp2(prefix_scores * factor - shift)
        suffix_exps = jnp.exp2(suffix_scores * factor - shift)
        total = jnp.sum(prefix_exps, axis=1, keepdims=True) + jnp.sum(suffix_exps, axis=1, keepdims=True)
        for half in range(2):
            copies[2 * group + half].wait()
        sums = jnp.dot(
            prefix_exps.astype(jnp.bfloat16), values_ref[0, :, lanes(group)], preferred_element_type=jnp.float32
        ) + jnp.dot(
            suffix_exps.astype(jnp.bfloat16), values_ref[1, :, lanes(group)], preferred_element_type=jnp.float32
        )
        share = sums * (1.0 / total)
        log_total = jnp.broadcast_to(shift + jnp.log2(total), (width, HD)).T[:STAT_ROWS]
        high, middle, low = split(log_total)
        stats = jnp.where(line == 0, high, jnp.where(line == 1, middle, jnp.where(line == 2, low, 0.0)))
        for head in range(per_group):
            first = head * rows
            tile = first // HD * HD
            stat = stats[:, tile : tile + HD]
            if first != tile:
                stat = pltpu.roll(stat, HD - (first - tile), 1)
            message = jnp.concatenate([share[first : first + rows], stat], 0)
            out_ref[group * per_group + head] = message.astype(jnp.bfloat16)

    held = scores(0)
    for group in range(KVH):
        following = scores(group + 1) if group + 1 < KVH else None
        weigh(group, *held)
        held = following


def attend(gathered, keys, prefix_cache, suffix_cache, mask):
    holders, rows, _ = gathered.shape
    tokens = prefix_cache.shape[1] + suffix_cache.shape[1]
    return pl.pallas_call(
        attend_kernel,
        in_specs=[
            pl.BlockSpec(memory_space=pltpu.VMEM),
            pl.BlockSpec(memory_space=pltpu.VMEM),
            pl.BlockSpec(memory_space=pltpu.HBM),
            pl.BlockSpec(memory_space=pltpu.HBM),
            pl.BlockSpec(memory_space=pltpu.VMEM),
        ],
        out_specs=pl.BlockSpec(memory_space=pltpu.VMEM),
        out_shape=jax.ShapeDtypeStruct((holders, rows + STAT_ROWS, HD), jnp.bfloat16),
        scratch_shapes=[
            pltpu.VMEM(suffix_cache.shape, suffix_cache.dtype),
            pltpu.SemaphoreType.DMA((2, KVH)),
        ],
        name="attend",
        compiler_params=pltpu.CompilerParams(vmem_limit_bytes=20 * MEGA),
        cost_estimate=pl.CostEstimate(
            flops=4 * H * rows * tokens * HD,
            bytes_accessed=5 * MEGA,
            transcendentals=H * rows * tokens,
        ),
    )(gathered, in_vmem(keys), in_hbm(prefix_cache), in_hbm(suffix_cache), mask)


def merge(received, rows):
    parts = received[:, rows : rows + 3, :rows].astype(jnp.float32)
    logs = parts[:, 0] + parts[:, 1] + parts[:, 2]
    factor = jnp.exp2(logs - jnp.max(logs, axis=0))
    merged = jnp.sum(received[:, :rows].astype(jnp.float32) * factor[..., None], axis=0)
    return merged / jnp.sum(factor, axis=0)[:, None]


def project_kernel(rows_ref, weight_ref, out_ref):
    steps = rows_ref.shape[0] // out_ref.shape[0]
    tile = 2 * steps
    pairs = rows_ref.shape[0] // tile
    columns = weight_ref.shape[1] // HD
    rows = rows_ref[...]
    lower = lax.broadcasted_iota(jnp.int32, (pairs, tile, HD), 1) < steps
    messages = [[], []]
    for pair in range(columns // 2):
        sums = jnp.dot(
            rows, weight_ref[:, pair * 2 * HD : (pair + 1) * 2 * HD], preferred_element_type=jnp.float32
        )
        even = sums[:, :HD].reshape(pairs, tile, HD)
        odd = sums[:, HD:].reshape(pairs, tile, HD)
        messages[0].append(jnp.where(lower, even, pltpu.roll(odd, steps, 1)))
        messages[1].append(jnp.where(lower, pltpu.roll(even, steps, 1), odd))
    for side in range(2):
        message = jnp.concatenate(messages[side], 1).astype(jnp.bfloat16)
        for pair in range(pairs):
            out_ref[pair * 2 + side] = message[pair]


def project(rows, weight, holders):
    lines = weight.shape[1] // HD * rows.shape[0] // holders
    return pl.pallas_call(
        project_kernel,
        out_shape=jax.ShapeDtypeStruct((holders, lines, HD), jnp.bfloat16),
        name="project",
        compiler_params=pltpu.CompilerParams(vmem_limit_bytes=16 * MEGA),
    )(rows, weight)


def suffix_mask(page_table, suffix_lengths, holder, slot_count, page_length, step_count):
    suffix_tokens = slot_count * page_length
    local_requests = page_table.shape[0]
    slot_ids = holder * slot_count + jnp.arange(slot_count, dtype=jnp.int32)
    matches = page_table[:, None, :] == slot_ids[None, :, None]
    ranks = jnp.arange(page_table.shape[1], dtype=jnp.int32) + 1
    held = jnp.max(jnp.where(matches, ranks, 0), axis=2)
    far = jnp.int32(1 << 30)
    starts = jnp.where(held > 0, (held - 1) * page_length, far)
    offsets = jnp.arange(page_length, dtype=jnp.int32)
    positions = (starts[:, :, None] + offsets).reshape(local_requests, 1, suffix_tokens)
    limits = suffix_lengths[:, None] + jnp.arange(step_count, dtype=jnp.int32)[None, :] + 1
    seen = positions < limits[:, :, None]
    mask = jnp.where(seen, 0.0, -jnp.inf).astype(jnp.float32)
    return mask.reshape(local_requests * step_count, suffix_tokens)


def body(queries, prefix_cache, suffix_pool, suffix_lengths, page_table, out_weight):
    step_count, local_requests, _ = queries.shape
    holders = lax.axis_size(PRE)
    gathered = exchange(spread(queries, holders), PRE)

    slot_count = suffix_pool.shape[1]
    page_length = suffix_pool.shape[2]
    holder = lax.axis_index("req") * holders + lax.axis_index(PRE)
    suffix_cache = suffix_pool.reshape(2, slot_count * page_length, KVH * HD)
    mask = suffix_mask(page_table, suffix_lengths, holder, slot_count, page_length, step_count)
    shares = attend(gathered, stage(prefix_cache, suffix_cache), prefix_cache, suffix_cache, mask)
    merged = merge(exchange(shares, PRE), step_count * local_requests)
    attended = jnp.transpose(merged.reshape(local_requests, step_count, HD), (1, 0, 2))
    copies = jnp.broadcast_to(merged.astype(jnp.bfloat16)[None], (lax.axis_size("req"),) + merged.shape)
    lines = exchange(copies, "req").reshape(-1, HD)
    pieces = exchange(project(lines, out_weight, holders), PRE)
    columns = out_weight.shape[1] // HD
    projected = jnp.sum(pieces.astype(jnp.float32), axis=0).reshape(columns, step_count, HD)
    projected = jnp.transpose(projected, (1, 0, 2)).reshape(step_count, columns * HD)
    return (attended, projected)


def solution(mesh):
    placed = (
        P(None, "req", PRE),
        P(None, PRE, None),
        P(None, ("req", PRE), None, None),
        P("req"),
        P("req", None),
        P(PRE, "req"),
    )
    return jax.shard_map(
        body,
        mesh=mesh,
        in_specs=placed,
        out_specs=(P(None, "req", PRE), P(PRE, "req")),
        check_vma=False,
    )
```

time: 113 us -> 107 us (0.947)
  local copies, waits for them, and re-layouts: 12.2 us -> 1.11 us
  Pallas kernels: 0 us -> 9.39 us
  matrix products: 6.7 us -> 0 us
  waiting for transfers between devices: 27.7 us -> 34.1 us
  other arithmetic: 6.44 us -> 3.15 us
    pallas_call x0 -> x4, Pallas kernels: none -> 9.39 us  [the longest x1 5.23 us: attend(): pl.pallas_call(attend_kernel, in_specs=[pl.BlockSpec(memory_space=pltpu.V...]
    dot_general x5 -> x0, matrix products: 6.7 us -> none  [the longest x2 4.7 us: weigh(): jnp.einsum('gmt,tgd->gmd', exps.astype(jnp.bfloat16), tiles, preferred_el...]
    all_to_all x2, waiting for transfers between devices: 27.7 us -> 34.1 us  [exchange(): return lax.all_to_all(blocks, axis, 0, 0, tiled=True)]
    unnamed x15 -> x3, local copies, waits for them, and re-layouts: 5.18 us -> 0.61 us
    slice x2 -> x0, local copies, waits for them, and re-layouts: 3.43 us -> none  [the longest x1 1.72 us: body(): prefix_cache[1]]
    reduce_sum x4 -> x2, other arithmetic: 3.47 us -> 0.37 us  [the longest x1 0.34 us: merge(): jnp.sum(received[:, :rows].astype(jnp.float32) * factor[..., None], axis=0)]
    reshape x2 -> x0, local copies, waits for them, and re-layouts: 1.34 us -> none  [the longest x1 1.13 us: body(): jnp.transpose(blocks, (0, 2, 1, 3))]
  transfers between devices with their start and end apart: 2 -> 2, of which waited for: 2 -> 2; matrix products, arithmetic and copies ran while one was open for 10% -> 3% of each run, Pallas kernels for 0% -> 1%
where the time goes in v2:
time: 107 us
  blocking collectives  36.6 us (34%)
  waiting for transfers between devices  34.1 us (32%)
  starting transfers between devices  21.8 us (20%)
  Pallas kernels  9.39 us (9%)
  other arithmetic  3.15 us (3%)
  local copies, waits for them, and re-layouts  1.11 us (1%)
    all_to_all x2, blocking collectives, exchange(): return lax.all_to_all(blocks, axis, 0, 0, tiled=True)  36.6 us
    all_to_all x2, waiting for transfers between devices, exchange(): return lax.all_to_all(blocks, axis, 0, 0, tiled=True)  34.1 us
    all_to_all x2, starting transfers between devices, exchange(): return lax.all_to_all(blocks, axis, 0, 0, tiled=True)  21.8 us
    pallas_call x1, Pallas kernels, attend(): pl.pallas_call(attend_kernel, in_specs=[pl.BlockSpec(memory_space=pltpu.V...  5.23 us
  transfers between devices with their start and end apart: 2, of which 2 were waited for; matrix products, arithmetic and copies ran while one was open for 3% of the time, Pallas kernels for 1%

profile of v2, /device:TPU:16, one launch (start us, length us, event | category | flops | bytes accessed | tf_op | source)
XLA Modules:
  0.0 106.9 jit_solution(1663083860779117202)
XLA Ops:
  0.6 1.5 %spread.1 = bf16[64,32,128]{2,1,0:T(8,128)(2,1)} custom-call(bf16[4,8,128]{2,1,0:T(8,128)(2,1)} %own_ref.1), custom_call_target="tpu_custom_call" | custom-call | tf_op jit(solution)/shard_map/spread/pallas_call | solution.py:47
  2.2 16.5 %all-to-all-start = ((bf16[64,32,128]{2,1,0:T(8,128)(2,1)}), bf16[64,32,128]{2,1,0:T(8,128)(2,1)S(1)}, u32[]{:S(2)}, u32[]{:S(2)}) async-start(bf16[64,32,128]{2,1,0:T(8,128)(2,1)} %spread.1), calls=%async_computation | async-start | bytes 1048576 | tf_op jit(solution)/shard_map/all_to_all | solution.py:19
  18.6 0.7 add_add_fusion
  19.4 0.1 add.112
  19.5 0.1 add.104
  19.6 1.0 select_reduce_fusion
  20.5 0.1 add.101
  20.6 0.1 add.102
  20.8 1.6 %stage.1.keys_ref = bf16[2,512,1024]{2,1,0:T(8,128)(2,1)S(1)} custom-call(bf16[2,512,1024]{2,1,0:T(8,128)(2,1)} %prefix_hbm.1, bf16[2,512,1024]{2,1,0:T(8,128)(2,1)} %bitcast.12), custom_call_target="tpu_custom_call" | custom-call | bytes 4194304 | tf_op jit(solution)/shard_map/stage/pallas_call | solution.py:68
  22.4 0.1 compare_select_fusion.mask_ref
  22.5 15.6 %all-to-all-done.query_ref = bf16[64,32,128]{2,1,0:T(8,128)(2,1)S(1)} async-done(((bf16[64,32,128]{2,1,0:T(8,128)(2,1)}), bf16[64,32,128]{2,1,0:T(8,128)(2,1)S(1)}, u32[]{:S(2)}, u32[]{:S(2)}) %all-to-all-start) | async-done | bytes 524320 | tf_op jit(solution)/shard_map/all_to_all | solution.py:19
  38.0 5.2 %attend.1 = bf16[64,40,128]{2,1,0:T(8,128)(2,1)S(1)} custom-call(bf16[64,32,128]{2,1,0:T(8,128)(2,1)S(1)} %all-to-all-done.query_ref, bf16[2,512,1024]{2,1,0:T(8,128)(2,1)S(1)} %stage.1.keys_ref, bf16[2,512,1024]{2,1,0:T(8,128)(2,1)} %prefix_hbm.1, bf16[2,512,1024]{2,1,0:T(8,128)(2,1)} %bitcast.13, f32[32,512]{1,0:T(8,128)S(1)} %compare_select_fusion.mask_ref), custom_call_target="tpu_custom_call" | custom-call | flops 1073741824 | bytes 5242880 | tf_op jit(solution)/shard_map/attend/pallas_call | solution.py:156
  43.3 26.9 %all_to_all.20 = bf16[64,40,128]{2,1,0:T(8,128)(2,1)S(1)} all-to-all(bf16[64,40,128]{2,1,0:T(8,128)(2,1)S(1)} %attend.1), channel_id=1, replica_groups=mesh['req'=8,'pre'=64] {'pre'}, dimensions={0} | all-to-all | bytes 1310720 | tf_op jit(solution)/shard_map/all_to_all | solution.py:19
  70.2 0.1 fusion.1
  70.3 0.3 multiply_reduce_fusion
  70.6 0.1 divide_convert_fusion
  70.7 9.7 %all_to_all.21 = bf16[8,32,128]{2,1,0:T(8,128)(2,1)S(1)} all-to-all(bf16[8,32,128]{2,1,0:T(8,128)(2,1)S(1)} %broadcast_in_dim.41), channel_id=1, replica_groups=mesh['req'=8,'pre'=64] {'req'}, dimensions={0} | all-to-all | bytes 131072 | tf_op jit(solution)/shard_map/all_to_all | solution.py:19
  80.5 1.1 %project.1 = bf16[64,32,128]{2,1,0:T(8,128)(2,1)} custom-call(bf16[256,128]{1,0:T(8,128)(2,1)S(1)} %bitcast.11, bf16[128,1024]{1,0:T(8,128)(2,1)S(1)} %copy-done), custom_call_target="tpu_custom_call" | custom-call | tf_op jit(solution)/shard_map/project/pallas_call | solution.py:213
  81.5 5.3 %all-to-all-start.3 = ((bf16[64,32,128]{2,1,0:T(8,128)(2,1)}), bf16[64,32,128]{2,1,0:T(8,128)(2,1)S(1)}, u32[]{:S(2)}, u32[]{:S(2)}) async-start(bf16[64,32,128]{2,1,0:T(8,128)(2,1)} %project.1), calls=%async_computation.3 | async-start | bytes 1048576 | tf_op jit(solution)/shard_map/all_to_all | solution.py:19
  86.9 0.1 div.19
  86.9 0.1 divide_bitcast_fusion
  87.0 0.6 copy.10
  87.6 18.5 %all-to-all-done.3 = bf16[64,32,128]{2,1,0:T(8,128)(2,1)S(1)} async-done(((bf16[64,32,128]{2,1,0:T(8,128)(2,1)}), bf16[64,32,128]{2,1,0:T(8,128)(2,1)S(1)}, u32[]{:S(2)}, u32[]{:S(2)}) %all-to-all-start.3) | async-done | bytes 524320 | tf_op jit(solution)/shard_map/all_to_all | solution.py:19
  106.2 0.7 convert_reduce_fusion
  (12 shorter events, 0.1 us)
Async XLA Ops:
  2.2 35.9 %all-to-all-start = ((bf16[64,32,128]{2,1,0:T(8,128)(2,1)}), bf16[64,32,128]{2,1,0:T(8,128)(2,1)S(1)}, u32[]{:S(2)}, u32[]{:S(2)}) async-start(bf16[64,32,128]{2,1,0:T(8,128)(2,1)} %spread.1), calls=%async_computation | async-start | bytes 1048576 | tf_op jit(solution)/shard_map/all_to_all | solution.py:19
  43.3 37.2 %copy-start = (bf16[128,1024]{1,0:T(8,128)(2,1)S(1)}, bf16[128,1024]{1,0:T(8,128)(2,1)}, u32[]{:S(2)}) copy-start(bf16[128,1024]{1,0:T(8,128)(2,1)} %weight_ref.1) | copy-start | bytes 786436
  81.5 24.6 %all-to-all-start.3 = ((bf16[64,32,128]{2,1,0:T(8,128)(2,1)}), bf16[64,32,128]{2,1,0:T(8,128)(2,1)S(1)}, u32[]{:S(2)}, u32[]{:S(2)}) async-start(bf16[64,32,128]{2,1,0:T(8,128)(2,1)} %project.1), calls=%async_computation.3 | async-start | bytes 1048576 | tf_op jit(solution)/shard_map/all_to_all | solution.py:19

commit v3 on v2

--- a/solution.py
+++ b/solution.py
@@ -5,14 +5,17 @@
 from jax import lax
 from jax.experimental import pallas as pl
 from jax.experimental.pallas import tpu as pltpu
+from jax.sharding import Mesh
 from jax.sharding import PartitionSpec as P
 
 H = 64
 KVH = 8
 HD = 128
 STAT_ROWS = 8
-PRE = "pre"
+PRE = ("y", "zh", "zl")
 MEGA = 1024 * 1024
+EARLY = 2
+LATE = ((2, 5), (5, 8))
 
 
 def exchange(blocks, axis):
@@ -53,11 +56,12 @@
     )(in_hbm(own))
 
 
-def stage_kernel(prefix_ref, suffix_ref, keys_ref, sems):
-    copies = [
-        pltpu.make_async_copy(prefix_ref.at[0], keys_ref.at[0], sems.at[0]),
-        pltpu.make_async_copy(suffix_ref.at[0], keys_ref.at[1], sems.at[1]),
-    ]
+def stage_kernel(prefix_ref, suffix_ref, keys_ref, values_ref, sems):
+    lanes = pl.ds(0, values_ref.shape[2])
+    copies = []
+    for half, cache in enumerate((prefix_ref, suffix_ref)):
+        copies.append(pltpu.make_async_copy(cache.at[0], keys_ref.at[half], sems.at[0, half]))
+        copies.append(pltpu.make_async_copy(cache.at[1, :, lanes], values_ref.at[half], sems.at[1, half]))
     for copy in copies:
         copy.start()
     for copy in copies:
@@ -65,15 +69,19 @@
 
 
 def stage(prefix_cache, suffix_cache):
+    halves, tokens, _ = prefix_cache.shape
     return pl.pallas_call(
         stage_kernel,
         in_specs=[pl.BlockSpec(memory_space=pl.ANY)] * 2,
-        out_specs=pl.BlockSpec(memory_space=pltpu.VMEM),
-        out_shape=pltpu.VMEM(prefix_cache.shape, prefix_cache.dtype),
-        scratch_shapes=[pltpu.SemaphoreType.DMA((2,))],
+        out_specs=[pl.BlockSpec(memory_space=pltpu.VMEM)] * 2,
+        out_shape=[
+            pltpu.VMEM(prefix_cache.shape, prefix_cache.dtype),
+            pltpu.VMEM((halves, tokens, EARLY * HD), prefix_cache.dtype),
+        ],
+        scratch_shapes=[pltpu.SemaphoreType.DMA((2, 2))],
         name="stage",
         compiler_params=pltpu.CompilerParams(vmem_limit_bytes=4 * MEGA),
-        cost_estimate=pl.CostEstimate(flops=0, bytes_accessed=4 * MEGA, transcendentals=0),
+        cost_estimate=pl.CostEstimate(flops=0, bytes_accessed=5 * MEGA, transcendentals=0),
     )(in_hbm(prefix_cache), in_hbm(suffix_cache))
 
 
@@ -84,7 +92,9 @@
     return high, middle, rest - middle
 
 
-def attend_kernel(query_ref, keys_ref, prefix_hbm, suffix_hbm, mask_ref, out_ref, values_ref, sems):
+def attend_kernel(
+    query_ref, keys_ref, early_ref, prefix_hbm, suffix_hbm, mask_ref, out_ref, values_ref, sems
+):
     rows = query_ref.shape[1]
     per_group = H // KVH
     width = per_group * rows
@@ -95,15 +105,15 @@
     def lanes(group):
         return slice(group * HD, (group + 1) * HD)
 
-    copies = []
-    for group in range(KVH):
-        part = pl.ds(group * HD, HD)
-        for half, cache in enumerate((prefix_hbm, suffix_hbm)):
-            copy = pltpu.make_async_copy(
-                cache.at[1, :, part], values_ref.at[half, :, part], sems.at[half, group]
-            )
+    copies = {}
+    for place, (first, last) in enumerate(LATE):
+        part = pl.ds(first * HD, (last - first) * HD)
+        copies[first] = [
+            pltpu.make_async_copy(cache.at[1, :, part], values_ref.at[half, :, part], sems.at[half, place])
+            for half, cache in enumerate((prefix_hbm, suffix_hbm))
+        ]
+        for copy in copies[first]:
             copy.start()
-            copies.append(copy)
 
     def scores(group):
         query = query_ref[group * per_group : (group + 1) * per_group].reshape(width, HD)
@@ -123,12 +133,13 @@
         prefix_exps = jnp.exp2(prefix_scores * factor - shift)
         suffix_exps = jnp.exp2(suffix_scores * factor - shift)
         total = jnp.sum(prefix_exps, axis=1, keepdims=True) + jnp.sum(suffix_exps, axis=1, keepdims=True)
-        for half in range(2):
-            copies[2 * group + half].wait()
+        for copy in copies.get(group, ()):
+            copy.wait()
+        source = early_ref if group < EARLY else values_ref
         sums = jnp.dot(
-            prefix_exps.astype(jnp.bfloat16), values_ref[0, :, lanes(group)], preferred_element_type=jnp.float32
+            prefix_exps.astype(jnp.bfloat16), source[0, :, lanes(group)], preferred_element_type=jnp.float32
         ) + jnp.dot(
-            suffix_exps.astype(jnp.bfloat16), values_ref[1, :, lanes(group)], preferred_element_type=jnp.float32
+            suffix_exps.astype(jnp.bfloat16), source[1, :, lanes(group)], preferred_element_type=jnp.float32
         )
         share = sums * (1.0 / total)
         log_total = jnp.broadcast_to(shift + jnp.log2(total), (width, HD)).T[:STAT_ROWS]
@@ -150,12 +161,13 @@
         held = following
 
 
-def attend(gathered, keys, prefix_cache, suffix_cache, mask):
+def attend(gathered, keys, early, prefix_cache, suffix_cache, mask):
     holders, rows, _ = gathered.shape
     tokens = prefix_cache.shape[1] + suffix_cache.shape[1]
     return pl.pallas_call(
         attend_kernel,
         in_specs=[
+            pl.BlockSpec(memory_space=pltpu.VMEM),
             pl.BlockSpec(memory_space=pltpu.VMEM),
             pl.BlockSpec(memory_space=pltpu.VMEM),
             pl.BlockSpec(memory_space=pltpu.HBM),
@@ -166,7 +178,7 @@
         out_shape=jax.ShapeDtypeStruct((holders, rows + STAT_ROWS, HD), jnp.bfloat16),
         scratch_shapes=[
             pltpu.VMEM(suffix_cache.shape, suffix_cache.dtype),
-            pltpu.SemaphoreType.DMA((2, KVH)),
+            pltpu.SemaphoreType.DMA((2, len(LATE))),
         ],
         name="attend",
         compiler_params=pltpu.CompilerParams(vmem_limit_bytes=20 * MEGA),
@@ -175,7 +187,7 @@
             bytes_accessed=5 * MEGA,
             transcendentals=H * rows * tokens,
         ),
-    )(gathered, in_vmem(keys), in_hbm(prefix_cache), in_hbm(suffix_cache), mask)
+    )(gathered, in_vmem(keys), in_vmem(early), in_hbm(prefix_cache), in_hbm(suffix_cache), mask)
 
 
 def merge(received, rows):
@@ -186,18 +198,23 @@
     return merged / jnp.sum(factor, axis=0)[:, None]
 
 
-def project_kernel(rows_ref, weight_ref, out_ref):
-    steps = rows_ref.shape[0] // out_ref.shape[0]
+def project_kernel(place_ref, rows_ref, own_ref, other_ref, out_ref):
+    groups, sides, lines, _ = rows_ref.shape
+    steps = groups * lines // out_ref.shape[0]
     tile = 2 * steps
-    pairs = rows_ref.shape[0] // tile
-    columns = weight_ref.shape[1] // HD
-    rows = rows_ref[...]
+    pairs = groups * lines // tile
+    columns = own_ref.shape[1] // HD
+    first, second = rows_ref[:, 0].reshape(groups * lines, HD), rows_ref[:, 1].reshape(groups * lines, HD)
+    here = jnp.full((groups * lines, HD), place_ref[0], jnp.int32) == 0
+    first, second = first.astype(jnp.float32), second.astype(jnp.float32)
+    rows = jnp.concatenate([jnp.where(here, first, second), jnp.where(here, second, first)], 1)
+    rows = rows.astype(jnp.bfloat16)
     lower = lax.broadcasted_iota(jnp.int32, (pairs, tile, HD), 1) < steps
     messages = [[], []]
     for pair in range(columns // 2):
-        sums = jnp.dot(
-            rows, weight_ref[:, pair * 2 * HD : (pair + 1) * 2 * HD], preferred_element_type=jnp.float32
-        )
+        part = slice(pair * 2 * HD, (pair + 1) * 2 * HD)
+        weight = jnp.concatenate([own_ref[:, part], other_ref[:, part]], 0)
+        sums = jnp.dot(rows, weight, preferred_element_type=jnp.float32)
         even = sums[:, :HD].reshape(pairs, tile, HD)
         odd = sums[:, HD:].reshape(pairs, tile, HD)
         messages[0].append(jnp.where(lower, even, pltpu.roll(odd, steps, 1)))
@@ -208,14 +225,16 @@
             out_ref[pair * 2 + side] = message[pair]
 
 
-def project(rows, weight, holders):
-    lines = weight.shape[1] // HD * rows.shape[0] // holders
+def project(rows, own, other, holders, place):
+    groups, sides, lines, _ = rows.shape
+    steps = groups * lines // holders
     return pl.pallas_call(
         project_kernel,
-        out_shape=jax.ShapeDtypeStruct((holders, lines, HD), jnp.bfloat16),
+        in_specs=[pl.BlockSpec(memory_space=pltpu.SMEM)] + [pl.BlockSpec(memory_space=pltpu.VMEM)] * 3,
+        out_shape=jax.ShapeDtypeStruct((holders, own.shape[1] // HD * steps, HD), jnp.bfloat16),
         name="project",
         compiler_params=pltpu.CompilerParams(vmem_limit_bytes=16 * MEGA),
-    )(rows, weight)
+    )(place, rows, own, other)
 
 
 def suffix_mask(page_table, suffix_lengths, holder, slot_count, page_length, step_count):
@@ -238,37 +257,47 @@
 def body(queries, prefix_cache, suffix_pool, suffix_lengths, page_table, out_weight):
     step_count, local_requests, _ = queries.shape
     holders = lax.axis_size(PRE)
-    gathered = exchange(spread(queries, holders), PRE)
-
+    outgoing = spread(queries, holders)
+    gathered = exchange(outgoing, PRE)
+
+    side = lax.axis_index("zl")
+    width = out_weight.shape[1] // 2
+    out_weight, outgoing = lax.optimization_barrier((out_weight, outgoing))
+    own_half = lax.dynamic_slice_in_dim(out_weight, side * width, width, 1)
+    other_half = lax.dynamic_slice_in_dim(out_weight, (1 - side) * width, width, 1)
+    other_half = lax.ppermute(other_half, "zl", [(0, 1), (1, 0)])
     slot_count = suffix_pool.shape[1]
     page_length = suffix_pool.shape[2]
     holder = lax.axis_index("req") * holders + lax.axis_index(PRE)
     suffix_cache = suffix_pool.reshape(2, slot_count * page_length, KVH * HD)
     mask = suffix_mask(page_table, suffix_lengths, holder, slot_count, page_length, step_count)
-    shares = attend(gathered, stage(prefix_cache, suffix_cache), prefix_cache, suffix_cache, mask)
+    shares = attend(gathered, *stage(prefix_cache, suffix_cache), prefix_cache, suffix_cache, mask)
+    shares, own_half, other_half = lax.optimization_barrier((shares, own_half, other_half))
     merged = merge(exchange(shares, PRE), step_count * local_requests)
     attended = jnp.transpose(merged.reshape(local_requests, step_count, HD), (1, 0, 2))
-    copies = jnp.broadcast_to(merged.astype(jnp.bfloat16)[None], (lax.axis_size("req"),) + merged.shape)
-    lines = exchange(copies, "req").reshape(-1, HD)
-    pieces = exchange(project(lines, out_weight, holders), PRE)
-    columns = out_weight.shape[1] // HD
-    projected = jnp.sum(pieces.astype(jnp.float32), axis=0).reshape(columns, step_count, HD)
-    projected = jnp.transpose(projected, (1, 0, 2)).reshape(step_count, columns * HD)
+    members = lax.axis_size("req")
+    copies = merged.astype(jnp.bfloat16)
+    copies = jnp.broadcast_to(copies[None], (2 * members,) + copies.shape)
+    lines = exchange(copies, ("req", "zl")).reshape((members, 2) + merged.shape)
+    pieces = exchange(project(lines, own_half, other_half, holders, side.reshape(1)), PRE)
+    sums = jnp.sum(pieces.astype(jnp.float32).reshape((-1, 2) + pieces.shape[1:]), axis=0)
+    projected = jnp.transpose(sums.reshape(-1, step_count, HD), (1, 0, 2)).reshape(step_count, -1)
     return (attended, projected)
 
 
 def solution(mesh):
+    fine = Mesh(mesh.devices.reshape(mesh.shape["req"], 8, 4, 2), ("req",) + PRE)
     placed = (
         P(None, "req", PRE),
         P(None, PRE, None),
-        P(None, ("req", PRE), None, None),
+        P(None, ("req",) + PRE, None, None),
         P("req"),
         P("req", None),
         P(PRE, "req"),
     )
     return jax.shard_map(
         body,
-        mesh=mesh,
+        mesh=fine,
         in_specs=placed,
         out_specs=(P(None, "req", PRE), P(PRE, "req")),
         check_vma=False,

time: 107 us -> 103 us (0.963)
  the two profiles are of different devices: /device:TPU:16 before, /device:TPU:2 now
where the time goes in v3:
time: 103 us; the launch traced here: 102 us
  blocking collectives  36.6 us (36%)
  starting transfers between devices  26.4 us (26%)
  waiting for transfers between devices  26 us (25%)
  Pallas kernels  8.2 us (8%)
  local copies, waits for them, and re-layouts  2.76 us (3%)
  other arithmetic  1.74 us (2%)
    all_to_all x2, blocking collectives, exchange(): return lax.all_to_all(blocks, axis, 0, 0, tiled=True)  36.6 us
    all_to_all x2, waiting for transfers between devices, exchange(): return lax.all_to_all(blocks, axis, 0, 0, tiled=True)  26 us
    all_to_all x2, starting transfers between devices, exchange(): return lax.all_to_all(blocks, axis, 0, 0, tiled=True)  22.9 us
    pallas_call x1, Pallas kernels, attend(): pl.pallas_call(attend_kernel, in_specs=[pl.BlockSpec(memory_space=pltpu.V...  4.04 us
    ppermute x1, starting transfers between devices, body(): other_half = lax.ppermute(other_half, 'zl', [(0, 1), (1, 0)])  3.47 us
  transfers between devices with their start and end apart: 3, of which 2 were waited for; matrix products, arithmetic and copies ran while one was open for 3% of the time, Pallas kernels for 6%

profile of v3, /device:TPU:2, one launch (start us, length us, event | category | flops | bytes accessed | tf_op | source)
XLA Modules:
  0.0 102.5 jit_solution(11902182759487813323)
XLA Ops:
  0.6 1.5 %spread.1 = bf16[64,32,128]{2,1,0:T(8,128)(2,1)} custom-call(bf16[4,8,128]{2,1,0:T(8,128)(2,1)} %own_ref.1), custom_call_target="tpu_custom_call" | custom-call | tf_op jit(solution)/shard_map/spread/pallas_call | solution.py:50
  2.2 16.6 %all-to-all-start = ((bf16[64,32,128]{2,1,0:T(8,128)(2,1)}), bf16[64,32,128]{2,1,0:T(8,128)(2,1)S(1)}, u32[]{:S(2)}, u32[]{:S(2)}) async-start(bf16[64,32,128]{2,1,0:T(8,128)(2,1)} %spread.1), calls=%async_computation | async-start | bytes 1048576 | tf_op jit(solution)/shard_map/all_to_all | solution.py:22
  18.8 1.6 %constant_dynamic-slice_fusion = (bf16[128,512]{1,0:T(8,128)(2,1)}, bf16[128,512]{1,0:T(8,128)(2,1)S(1)}) fusion(bf16[128,1024]{1,0:T(8,128)(2,1)} %param.11, s32[]{:T(128)S(6)} %select_n.27, s32[]{:T(128)S(6)} %select_n.26), kind=kLoop, calls=%fused_computation.14 | loop fusion | bytes 524296 | tf_op jit(solution)/shard_map/dynamic_slice | solution.py:267
  20.4 3.5 %collective-permute-start = (bf16[128,512]{1,0:T(8,128)(2,1)}, bf16[128,512]{1,0:T(8,128)(2,1)S(1)}, u32[]{:S(2)}, u32[]{:S(2)}) collective-permute-start(bf16[128,512]{1,0:T(8,128)(2,1)} %get-tuple-element.22), channel_id=1, source_target_pairs={{0,1},{1,0},{2,3},{3,2},{4,5},{5,4},{6,7},{7,6},{8,9},{9,8},{10,11... | collective-permute-start | bytes 393224 | tf_op jit(solution)/shard_map/ppermute | solution.py:268
  24.0 0.1 add.126
  24.1 0.1 add.118
  24.2 0.3 select_reduce_fusion
  24.5 0.1 add.115
  24.6 0.1 add.116
  24.8 1.7 %stage.1 = (bf16[2,512,1024]{2,1,0:T(8,128)(2,1)S(1)}, bf16[2,512,256]{2,1,0:T(8,128)(2,1)S(1)}) custom-call(bf16[2,512,1024]{2,1,0:T(8,128)(2,1)} %prefix_hbm.1, bf16[2,512,1024]{2,1,0:T(8,128)(2,1)} %bitcast.15), custom_call_target="tpu_custom_call" | custom-call | bytes 5242880 | tf_op jit(solution)/shard_map/stage/pallas_call | solution.py:73
  26.5 11.5 %all-to-all-done.query_ref = bf16[64,32,128]{2,1,0:T(8,128)(2,1)S(1)} async-done(((bf16[64,32,128]{2,1,0:T(8,128)(2,1)}), bf16[64,32,128]{2,1,0:T(8,128)(2,1)S(1)}, u32[]{:S(2)}, u32[]{:S(2)}) %all-to-all-start) | async-done | bytes 524320 | tf_op jit(solution)/shard_map/all_to_all | solution.py:22
  38.1 4.0 %attend.1 = bf16[64,40,128]{2,1,0:T(8,128)(2,1)S(1)} custom-call(bf16[64,32,128]{2,1,0:T(8,128)(2,1)S(1)} %all-to-all-done.query_ref, bf16[2,512,1024]{2,1,0:T(8,128)(2,1)S(1)} %get-tuple-element.8.keys_ref, bf16[2,512,256]{2,1,0:T(8,128)(2,1)S(1)} %get-tuple-element.9.early_ref, bf16[2,512,1024]{2,1,0:T(8,128)(2,1)} %prefix_hbm.1, ...), custom_call_target="tpu_custom_call" | custom-call | flops 1073741824 | bytes 5242880 | tf_op jit(solution)/shard_map/attend/pallas_call | solution.py:167
  42.1 26.2 %all_to_all.20 = bf16[64,40,128]{2,1,0:T(8,128)(2,1)S(1)} all-to-all(bf16[64,40,128]{2,1,0:T(8,128)(2,1)S(1)} %attend.1), channel_id=1, replica_groups=mesh['req'=8,'y'=8,'zh'=4,'zl'=2] {'y','zh','zl'}, dimensions={0} | all-to-all | bytes 1310720 | tf_op jit(solution)/shard_map/all_to_all | solution.py:22
  68.4 0.1 fusion.1
  68.5 0.3 multiply_reduce_fusion
  68.9 0.1 divide_convert_fusion
  69.0 10.4 %all_to_all.21 = bf16[16,32,128]{2,1,0:T(8,128)(2,1)S(1)} all-to-all(bf16[16,32,128]{2,1,0:T(8,128)(2,1)S(1)} %broadcast_in_dim.41), channel_id=1, replica_groups=mesh['req'=8,'y'=8,'zh'=4,'zl'=2] {'req','zl'}, dimensions={0} | all-to-all | bytes 262144 | tf_op jit(solution)/shard_map/all_to_all | solution.py:22
  79.3 0.9 project.1
  80.3 6.3 %all-to-all-start.3 = ((bf16[64,16,128]{2,1,0:T(8,128)(2,1)}), bf16[64,16,128]{2,1,0:T(8,128)(2,1)S(1)}, u32[]{:S(2)}, u32[]{:S(2)}) async-start(bf16[64,16,128]{2,1,0:T(8,128)(2,1)} %project.1), calls=%async_computation.3 | async-start | bytes 524288 | tf_op jit(solution)/shard_map/all_to_all | solution.py:22
  86.6 0.1 div.19
  86.7 0.1 divide_bitcast_fusion
  86.7 0.6 copy.10
  87.4 14.5 %all-to-all-done.3 = bf16[64,16,128]{2,1,0:T(8,128)(2,1)S(1)} async-done(((bf16[64,16,128]{2,1,0:T(8,128)(2,1)}), bf16[64,16,128]{2,1,0:T(8,128)(2,1)S(1)}, u32[]{:S(2)}, u32[]{:S(2)}) %all-to-all-start.3) | async-done | bytes 262176 | tf_op jit(solution)/shard_map/all_to_all | solution.py:22
  101.8 0.7 convert_reduce_fusion
  (17 shorter events, 0.3 us)
Async XLA Ops:
  0.6 23.3 %copy-start.1 = (s32[8]{0:T(128)S(1)}, s32[8]{0:T(128)}, u32[]{:S(2)}) copy-start(s32[8]{0:T(128)} %param.9) | copy-start | bytes 100
  0.6 23.5 %copy-start = (s32[8,256]{1,0:T(8,128)S(1)}, s32[8,256]{1,0:T(8,128)}, u32[]{:S(2)}) copy-start(s32[8,256]{1,0:T(8,128)} %param.10) | copy-start | bytes 24580
  2.2 35.9 %all-to-all-start = ((bf16[64,32,128]{2,1,0:T(8,128)(2,1)}), bf16[64,32,128]{2,1,0:T(8,128)(2,1)S(1)}, u32[]{:S(2)}, u32[]{:S(2)}) async-start(bf16[64,32,128]{2,1,0:T(8,128)(2,1)} %spread.1), calls=%async_computation | async-start | bytes 1048576 | tf_op jit(solution)/shard_map/all_to_all | solution.py:22
  20.4 21.7 %collective-permute-start = (bf16[128,512]{1,0:T(8,128)(2,1)}, bf16[128,512]{1,0:T(8,128)(2,1)S(1)}, u32[]{:S(2)}, u32[]{:S(2)}) collective-permute-start(bf16[128,512]{1,0:T(8,128)(2,1)} %get-tuple-element.22), channel_id=1, source_target_pairs={{0,1},{1,0},{2,3},{3,2},{4,5},{5,4},{6,7},{7,6},{8,9},{9,8},{10,11... | collective-permute-start | bytes 393224 | tf_op jit(solution)/shard_map/ppermute | solution.py:268
  80.3 21.6 %all-to-all-start.3 = ((bf16[64,16,128]{2,1,0:T(8,128)(2,1)}), bf16[64,16,128]{2,1,0:T(8,128)(2,1)S(1)}, u32[]{:S(2)}, u32[]{:S(2)}) async-start(bf16[64,16,128]{2,1,0:T(8,128)(2,1)} %project.1), calls=%async_computation.3 | async-start | bytes 524288 | tf_op jit(solution)/shard_map/all_to_all | solution.py:22

commit v4 on v3

--- a/solution.py
+++ b/solution.py
@@ -12,6 +12,7 @@
 KVH = 8
 HD = 128
 STAT_ROWS = 8
+SPARE = 2
 PRE = ("y", "zh", "zl")
 MEGA = 1024 * 1024
 EARLY = 2
@@ -53,7 +54,7 @@
         out_shape=pltpu.VMEM((holders, rows, HD), own.dtype),
         name="spread",
         compiler_params=pltpu.CompilerParams(vmem_limit_bytes=4 * MEGA),
-    )(in_hbm(own))
+    )(own)
 
 
 def stage_kernel(prefix_ref, suffix_ref, keys_ref, values_ref, sems):
@@ -98,7 +99,7 @@
     rows = query_ref.shape[1]
     per_group = H // KVH
     width = per_group * rows
-    line = lax.broadcasted_iota(jnp.int32, (STAT_ROWS, width), 0)
+    lane_group = lax.broadcasted_iota(jnp.int32, (STAT_ROWS, HD), 1) // rows
     factor = math.log2(math.e) / math.sqrt(HD)
     suffix_tokens = mask_ref.shape[1]
 
@@ -144,15 +145,18 @@
         share = sums * (1.0 / total)
         log_total = jnp.broadcast_to(shift + jnp.log2(total), (width, HD)).T[:STAT_ROWS]
         high, middle, low = split(log_total)
-        stats = jnp.where(line == 0, high, jnp.where(line == 1, middle, jnp.where(line == 2, low, 0.0)))
+        pieces = []
         for head in range(per_group):
             first = head * rows
             tile = first // HD * HD
-            stat = stats[:, tile : tile + HD]
-            if first != tile:
-                stat = pltpu.roll(stat, HD - (first - tile), 1)
-            message = jnp.concatenate([share[first : first + rows], stat], 0)
-            out_ref[group * per_group + head] = message.astype(jnp.bfloat16)
+            stat = jnp.zeros((STAT_ROWS, HD), jnp.float32)
+            for place, part in enumerate((high, middle, low)):
+                turn = (place * rows + tile - first) % HD
+                part = part[:, tile : tile + HD]
+                stat = jnp.where(lane_group == place, pltpu.roll(part, turn, 1) if turn else part, stat)
+            pieces += [share[first : first + rows], stat[:SPARE]]
+        lines = per_group * (rows + SPARE)
+        out_ref[group * lines : (group + 1) * lines] = jnp.concatenate(pieces, 0).astype(jnp.bfloat16)
 
     held = scores(0)
     for group in range(KVH):
@@ -175,7 +179,7 @@
             pl.BlockSpec(memory_space=pltpu.VMEM),
         ],
         out_specs=pl.BlockSpec(memory_space=pltpu.VMEM),
-        out_shape=jax.ShapeDtypeStruct((holders, rows + STAT_ROWS, HD), jnp.bfloat16),
+        out_shape=jax.ShapeDtypeStruct((holders * (rows + SPARE), HD), jnp.bfloat16),
         scratch_shapes=[
             pltpu.VMEM(suffix_cache.shape, suffix_cache.dtype),
             pltpu.SemaphoreType.DMA((2, len(LATE))),
@@ -190,12 +194,61 @@
     )(gathered, in_vmem(keys), in_vmem(early), in_hbm(prefix_cache), in_hbm(suffix_cache), mask)
 
 
-def merge(received, rows):
-    parts = received[:, rows : rows + 3, :rows].astype(jnp.float32)
-    logs = parts[:, 0] + parts[:, 1] + parts[:, 2]
-    factor = jnp.exp2(logs - jnp.max(logs, axis=0))
-    merged = jnp.sum(received[:, :rows].astype(jnp.float32) * factor[..., None], axis=0)
-    return merged / jnp.sum(factor, axis=0)[:, None]
+def merge_kernel(received_ref, merged_ref, copies_ref):
+    rows = merged_ref.shape[0]
+    lines = rows + SPARE
+    holders = received_ref.shape[0] // lines
+    tiles = received_ref.shape[0] // HD
+    stats = []
+    for holder in range(holders):
+        place = holder * lines + rows
+        base = place // 16 * 16
+        stats.append(received_ref[base : base + 16].astype(jnp.float32)[place - base : place - base + 1])
+    stats = jnp.concatenate(stats, 0)
+    log_totals = stats + pltpu.roll(stats, HD - rows, 1) + pltpu.roll(stats, HD - 2 * rows, 1)
+    factors = jnp.exp2(log_totals - jnp.max(log_totals, axis=0, keepdims=True))
+    factors = factors * (1.0 / jnp.sum(factors, axis=0, keepdims=True))
+    lane = lax.broadcasted_iota(jnp.int32, (STAT_ROWS, HD), 1)
+    spans = [jnp.zeros((STAT_ROWS, HD), jnp.float32) for _ in range(tiles)]
+    for holder in range(holders):
+        tile, turn = divmod(holder * lines, HD)
+        factor = jnp.broadcast_to(factors[holder : holder + 1], (STAT_ROWS, HD))
+        if turn:
+            factor = pltpu.roll(factor, turn, 1)
+        spans[tile] = jnp.where((lane >= turn) & (lane < turn + rows), factor, spans[tile])
+        if turn + rows > HD:
+            spans[tile + 1] = jnp.where(lane < turn + rows - HD, factor, spans[tile + 1])
+    row = lax.broadcasted_iota(jnp.int32, (rows, HD), 0)
+    column = lax.broadcasted_iota(jnp.int32, (rows, HD), 1)
+    weights = jnp.concatenate(
+        [
+            jnp.where(
+                lax.rem(column + tile * HD, lines) == row, jnp.broadcast_to(spans[tile][:1], (rows, HD)), 0.0
+            )
+            for tile in range(tiles)
+        ],
+        1,
+    )
+    high = weights.astype(jnp.bfloat16)
+    low = (weights - high.astype(jnp.float32)).astype(jnp.bfloat16)
+    sums = jnp.dot(jnp.concatenate([high, low], 0), received_ref[...], preferred_element_type=jnp.float32)
+    merged = sums[:rows] + sums[rows:]
+    merged_ref[...] = merged
+    rounded = merged.astype(jnp.bfloat16)
+    for copy in range(copies_ref.shape[0]):
+        copies_ref[copy] = rounded
+
+
+def merge(received, rows, copies):
+    return pl.pallas_call(
+        merge_kernel,
+        out_shape=[
+            jax.ShapeDtypeStruct((rows, HD), jnp.float32),
+            jax.ShapeDtypeStruct((copies, rows, HD), jnp.bfloat16),
+        ],
+        name="merge",
+        compiler_params=pltpu.CompilerParams(vmem_limit_bytes=16 * MEGA),
+    )(received)
 
 
 def project_kernel(place_ref, rows_ref, own_ref, other_ref, out_ref):
@@ -234,7 +287,7 @@
         out_shape=jax.ShapeDtypeStruct((holders, own.shape[1] // HD * steps, HD), jnp.bfloat16),
         name="project",
         compiler_params=pltpu.CompilerParams(vmem_limit_bytes=16 * MEGA),
-    )(place, rows, own, other)
+    )(place, rows, in_vmem(own), in_vmem(other))
 
 
 def suffix_mask(page_table, suffix_lengths, holder, slot_count, page_length, step_count):
@@ -273,11 +326,12 @@
     mask = suffix_mask(page_table, suffix_lengths, holder, slot_count, page_length, step_count)
     shares = attend(gathered, *stage(prefix_cache, suffix_cache), prefix_cache, suffix_cache, mask)
     shares, own_half, other_half = lax.optimization_barrier((shares, own_half, other_half))
-    merged = merge(exchange(shares, PRE), step_count * local_requests)
+    rows = step_count * local_requests
+    members = lax.axis_size("req")
+    shape = shares.shape
+    shares = exchange(shares.reshape(holders, -1, SPARE, HD), PRE).reshape(shape)
+    merged, copies = merge(shares, rows, 2 * members)
     attended = jnp.transpose(merged.reshape(local_requests, step_count, HD), (1, 0, 2))
-    members = lax.axis_size("req")
-    copies = merged.astype(jnp.bfloat16)
-    copies = jnp.broadcast_to(copies[None], (2 * members,) + copies.shape)
     lines = exchange(copies, ("req", "zl")).reshape((members, 2) + merged.shape)
     pieces = exchange(project(lines, own_half, other_half, holders, side.reshape(1)), PRE)
     sums = jnp.sum(pieces.astype(jnp.float32).reshape((-1, 2) + pieces.shape[1:]), axis=0)

time: 103 us -> 101 us (0.981)
  blocking collectives: 36.6 us -> 34.9 us
    all_to_all x2, blocking collectives: 36.6 us -> 34.9 us  [exchange(): return lax.all_to_all(blocks, axis, 0, 0, tiled=True)]
  transfers between devices with their start and end apart: 3 -> 3, of which waited for: 2 -> 2; matrix products, arithmetic and copies ran while one was open for 3% -> 3% of each run, Pallas kernels for 6% -> 7%
where the time goes in v4:
time: 101 us
  blocking collectives  34.9 us (35%)
  waiting for transfers between devices  26.2 us (26%)
  starting transfers between devices  25.9 us (26%)
  Pallas kernels  8.78 us (9%)
  local copies, waits for them, and re-layouts  3.35 us (3%)
  other arithmetic  1.09 us (1%)
    all_to_all x2, blocking collectives, exchange(): return lax.all_to_all(blocks, axis, 0, 0, tiled=True)  34.9 us
    all_to_all x2, waiting for transfers between devices, exchange(): return lax.all_to_all(blocks, axis, 0, 0, tiled=True)  26.2 us
    all_to_all x2, starting transfers between devices, exchange(): return lax.all_to_all(blocks, axis, 0, 0, tiled=True)  22.4 us
    pallas_call x1, Pallas kernels, attend(): pl.pallas_call(attend_kernel, in_specs=[pl.BlockSpec(memory_space=pltpu.V...  4.87 us
    ppermute x1, starting transfers between devices, body(): other_half = lax.ppermute(other_half, 'zl', [(0, 1), (1, 0)])  3.47 us
  transfers between devices with their start and end apart: 3, of which 2 were waited for; matrix products, arithmetic and copies ran while one was open for 3% of the time, Pallas kernels for 7%

profile of v4, /device:TPU:2, one launch (start us, length us, event | category | flops | bytes accessed | tf_op | source)
XLA Modules:
  0.0 101.0 jit_solution(9891456332603926237)
XLA Ops:
  0.6 0.7 copy-done
  1.3 0.8 spread.1
  2.2 16.6 %all-to-all-start = ((bf16[64,32,128]{2,1,0:T(8,128)(2,1)}), bf16[64,32,128]{2,1,0:T(8,128)(2,1)S(1)}, u32[]{:S(2)}, u32[]{:S(2)}) async-start(bf16[64,32,128]{2,1,0:T(8,128)(2,1)} %spread.1), calls=%async_computation | async-start | bytes 1048576 | tf_op jit(solution)/shard_map/all_to_all | solution.py:23
  18.8 1.6 %constant_dynamic-slice_fusion = (bf16[128,512]{1,0:T(8,128)(2,1)}, bf16[128,512]{1,0:T(8,128)(2,1)S(1)}) fusion(bf16[128,1024]{1,0:T(8,128)(2,1)} %param.11, s32[]{:T(128)S(6)} %select_n.27, s32[]{:T(128)S(6)} %select_n.26), kind=kLoop, calls=%fused_computation.8 | loop fusion | bytes 524296 | tf_op jit(solution)/shard_map/dynamic_slice | solution.py:320
  20.4 3.5 %collective-permute-start = (bf16[128,512]{1,0:T(8,128)(2,1)}, bf16[128,512]{1,0:T(8,128)(2,1)S(1)}, u32[]{:S(2)}, u32[]{:S(2)}) collective-permute-start(bf16[128,512]{1,0:T(8,128)(2,1)} %get-tuple-element.18), channel_id=1, source_target_pairs={{0,1},{1,0},{2,3},{3,2},{4,5},{5,4},{6,7},{7,6},{8,9},{9,8},{10,11... | collective-permute-start | bytes 393224 | tf_op jit(solution)/shard_map/ppermute | solution.py:321
  23.9 0.1 add_add_fusion
  24.0 0.1 add.108
  24.0 0.1 add.100
  24.2 0.3 select_reduce_fusion
  24.4 0.1 add.97
  24.5 0.1 add.98
  24.7 0.1 compare_select_fusion.mask_ref
  24.8 1.7 %stage.1 = (bf16[2,512,1024]{2,1,0:T(8,128)(2,1)S(1)}, bf16[2,512,256]{2,1,0:T(8,128)(2,1)S(1)}) custom-call(bf16[2,512,1024]{2,1,0:T(8,128)(2,1)} %prefix_hbm.1, bf16[2,512,1024]{2,1,0:T(8,128)(2,1)} %bitcast.20), custom_call_target="tpu_custom_call" | custom-call | bytes 5242880 | tf_op jit(solution)/shard_map/stage/pallas_call | solution.py:74
  26.5 11.5 %all-to-all-done.query_ref = bf16[64,32,128]{2,1,0:T(8,128)(2,1)S(1)} async-done(((bf16[64,32,128]{2,1,0:T(8,128)(2,1)}), bf16[64,32,128]{2,1,0:T(8,128)(2,1)S(1)}, u32[]{:S(2)}, u32[]{:S(2)}) %all-to-all-start) | async-done | bytes 524320 | tf_op jit(solution)/shard_map/all_to_all | solution.py:23
  38.0 4.9 %attend.1 = bf16[2176,128]{1,0:T(8,128)(2,1)S(1)} custom-call(bf16[64,32,128]{2,1,0:T(8,128)(2,1)S(1)} %all-to-all-done.query_ref, bf16[2,512,1024]{2,1,0:T(8,128)(2,1)S(1)} %get-tuple-element.10.keys_ref, bf16[2,512,256]{2,1,0:T(8,128)(2,1)S(1)} %get-tuple-element.11.early_ref, bf16[2,512,1024]{2,1,0:T(8,128)(2,1)} %prefix_hbm.1, ...), custom_call_target="tpu_custom_call" | custom-call | flops 1073741824 | bytes 5242880 | tf_op jit(solution)/shard_map/attend/pallas_call | solution.py:171
  42.9 0.0 collective-permute-done.other_ref
  42.9 24.5 %all_to_all.20 = bf16[64,17,2,128]{3,2,1,0:T(2,128)(2,1)S(1)} all-to-all(bf16[64,17,2,128]{3,2,1,0:T(2,128)(2,1)S(1)} %bitcast.17), channel_id=1, replica_groups=mesh['req'=8,'y'=8,'zh'=4,'zl'=2] {'y','zh','zl'}, dimensions={0} | all-to-all | bytes 1114112 | tf_op jit(solution)/shard_map/all_to_all | solution.py:23
  67.5 0.4 merge.1
  67.9 10.4 %all_to_all.21 = bf16[16,32,128]{2,1,0:T(8,128)(2,1)S(1)} all-to-all(bf16[16,32,128]{2,1,0:T(8,128)(2,1)S(1)} %get-tuple-element.15), channel_id=1, replica_groups=mesh['req'=8,'y'=8,'zh'=4,'zl'=2] {'req','zl'}, dimensions={0} | all-to-all | bytes 262144 | tf_op jit(solution)/shard_map/all_to_all | solution.py:23
  78.3 0.9 project.1
  79.2 5.9 %all-to-all-start.3 = ((bf16[64,16,128]{2,1,0:T(8,128)(2,1)}), bf16[64,16,128]{2,1,0:T(8,128)(2,1)S(1)}, u32[]{:S(2)}, u32[]{:S(2)}) async-start(bf16[64,16,128]{2,1,0:T(8,128)(2,1)} %project.1), calls=%async_computation.3 | async-start | bytes 524288 | tf_op jit(solution)/shard_map/all_to_all | solution.py:23
  85.1 0.6 copy.12
  85.7 14.6 %all-to-all-done.3 = bf16[64,16,128]{2,1,0:T(8,128)(2,1)S(1)} async-done(((bf16[64,16,128]{2,1,0:T(8,128)(2,1)}), bf16[64,16,128]{2,1,0:T(8,128)(2,1)S(1)}, u32[]{:S(2)}, u32[]{:S(2)}) %all-to-all-start.3) | async-done | bytes 262176 | tf_op jit(solution)/shard_map/all_to_all | solution.py:23
  100.4 0.7 convert_reduce_fusion
  (12 shorter events, 0.1 us)
Async XLA Ops:
  0.6 0.7 copy-start
  1.3 22.5 %copy-start.2 = (s32[8]{0:T(128)S(1)}, s32[8]{0:T(128)}, u32[]{:S(2)}) copy-start(s32[8]{0:T(128)} %param.9) | copy-start | bytes 100
  1.3 22.8 %copy-start.1 = (s32[8,256]{1,0:T(8,128)S(1)}, s32[8,256]{1,0:T(8,128)}, u32[]{:S(2)}) copy-start(s32[8,256]{1,0:T(8,128)} %param.10) | copy-start | bytes 24580
  2.2 35.9 %all-to-all-start = ((bf16[64,32,128]{2,1,0:T(8,128)(2,1)}), bf16[64,32,128]{2,1,0:T(8,128)(2,1)S(1)}, u32[]{:S(2)}, u32[]{:S(2)}) async-start(bf16[64,32,128]{2,1,0:T(8,128)(2,1)} %spread.1), calls=%async_computation | async-start | bytes 1048576 | tf_op jit(solution)/shard_map/all_to_all | solution.py:23
  20.4 22.5 %collective-permute-start = (bf16[128,512]{1,0:T(8,128)(2,1)}, bf16[128,512]{1,0:T(8,128)(2,1)S(1)}, u32[]{:S(2)}, u32[]{:S(2)}) collective-permute-start(bf16[128,512]{1,0:T(8,128)(2,1)} %get-tuple-element.18), channel_id=1, source_target_pairs={{0,1},{1,0},{2,3},{3,2},{4,5},{5,4},{6,7},{7,6},{8,9},{9,8},{10,11... | collective-permute-start | bytes 393224 | tf_op jit(solution)/shard_map/ppermute | solution.py:321
  79.2 21.1 %all-to-all-start.3 = ((bf16[64,16,128]{2,1,0:T(8,128)(2,1)}), bf16[64,16,128]{2,1,0:T(8,128)(2,1)S(1)}, u32[]{:S(2)}, u32[]{:S(2)}) async-start(bf16[64,16,128]{2,1,0:T(8,128)(2,1)} %project.1), calls=%async_computation.3 | async-start | bytes 524288 | tf_op jit(solution)/shard_map/all_to_all | solution.py:23

commit v5 on v4

--- a/solution.py
+++ b/solution.py
@@ -116,6 +116,9 @@
         for copy in copies[first]:
             copy.start()
 
+    def with_ones(values):
+        return jnp.concatenate([values, jnp.ones(values.shape, values.dtype)], 1)
+
     def scores(group):
         query = query_ref[group * per_group : (group + 1) * per_group].reshape(width, HD)
 
@@ -133,17 +136,17 @@
         shift = row_max * factor
         prefix_exps = jnp.exp2(prefix_scores * factor - shift)
         suffix_exps = jnp.exp2(suffix_scores * factor - shift)
-        total = jnp.sum(prefix_exps, axis=1, keepdims=True) + jnp.sum(suffix_exps, axis=1, keepdims=True)
         for copy in copies.get(group, ()):
             copy.wait()
         source = early_ref if group < EARLY else values_ref
         sums = jnp.dot(
-            prefix_exps.astype(jnp.bfloat16), source[0, :, lanes(group)], preferred_element_type=jnp.float32
+            prefix_exps.astype(jnp.bfloat16), with_ones(source[0, :, lanes(group)]), preferred_element_type=jnp.float32
         ) + jnp.dot(
-            suffix_exps.astype(jnp.bfloat16), source[1, :, lanes(group)], preferred_element_type=jnp.float32
+            suffix_exps.astype(jnp.bfloat16), with_ones(source[1, :, lanes(group)]), preferred_element_type=jnp.float32
         )
+        sums, total = sums[:, :HD], sums[:, HD:]
         share = sums * (1.0 / total)
-        log_total = jnp.broadcast_to(shift + jnp.log2(total), (width, HD)).T[:STAT_ROWS]
+        log_total = (shift + jnp.log2(total)).T[:STAT_ROWS]
         high, middle, low = split(log_total)
         pieces = []
         for head in range(per_group):

time: 101 us -> 100 us (0.990)
  Pallas kernels: 8.78 us -> 7.59 us
    pallas_call x1, Pallas kernels: 4.87 us -> 3.69 us  [attend(): pl.pallas_call(attend_kernel, in_specs=[pl.BlockSpec(memory_space=pltpu.V...]
  transfers between devices with their start and end apart: 3 -> 3, of which waited for: 2 -> 2; matrix products, arithmetic and copies ran while one was open for 3% -> 3% of each run, Pallas kernels for 7% -> 5%
where the time goes in v5:
time: 100 us; the launch traced here: 99.8 us
  blocking collectives  34.9 us (35%)
  waiting for transfers between devices  26.2 us (26%)
  starting transfers between devices  25.9 us (26%)
  Pallas kernels  7.59 us (8%)
  local copies, waits for them, and re-layouts  3.35 us (3%)
  other arithmetic  1.09 us (1%)
    all_to_all x2, blocking collectives, exchange(): return lax.all_to_all(blocks, axis, 0, 0, tiled=True)  34.9 us
    all_to_all x2, waiting for transfers between devices, exchange(): return lax.all_to_all(blocks, axis, 0, 0, tiled=True)  26.2 us
    all_to_all x2, starting transfers between devices, exchange(): return lax.all_to_all(blocks, axis, 0, 0, tiled=True)  22.5 us
    pallas_call x1, Pallas kernels, attend(): pl.pallas_call(attend_kernel, in_specs=[pl.BlockSpec(memory_space=pltpu.V...  3.69 us
    ppermute x1, starting transfers between devices, body(): other_half = lax.ppermute(other_half, 'zl', [(0, 1), (1, 0)])  3.47 us
  transfers between devices with their start and end apart: 3, of which 2 were waited for; matrix products, arithmetic and copies ran while one was open for 3% of the time, Pallas kernels for 5%

profile of v5, /device:TPU:2, one launch (start us, length us, event | category | flops | bytes accessed | tf_op | source)
XLA Modules:
  0.0 99.8 jit_solution(1134777094933765902)
XLA Ops:
  0.6 0.7 copy-done
  1.3 0.8 spread.1
  2.2 16.6 %all-to-all-start = ((bf16[64,32,128]{2,1,0:T(8,128)(2,1)}), bf16[64,32,128]{2,1,0:T(8,128)(2,1)S(1)}, u32[]{:S(2)}, u32[]{:S(2)}) async-start(bf16[64,32,128]{2,1,0:T(8,128)(2,1)} %spread.1), calls=%async_computation | async-start | bytes 1048576 | tf_op jit(solution)/shard_map/all_to_all | solution.py:23
  18.8 1.6 %constant_dynamic-slice_fusion = (bf16[128,512]{1,0:T(8,128)(2,1)}, bf16[128,512]{1,0:T(8,128)(2,1)S(1)}) fusion(bf16[128,1024]{1,0:T(8,128)(2,1)} %param.11, s32[]{:T(128)S(6)} %select_n.27, s32[]{:T(128)S(6)} %select_n.26), kind=kLoop, calls=%fused_computation.8 | loop fusion | bytes 524296 | tf_op jit(solution)/shard_map/dynamic_slice | solution.py:323
  20.4 3.5 %collective-permute-start = (bf16[128,512]{1,0:T(8,128)(2,1)}, bf16[128,512]{1,0:T(8,128)(2,1)S(1)}, u32[]{:S(2)}, u32[]{:S(2)}) collective-permute-start(bf16[128,512]{1,0:T(8,128)(2,1)} %get-tuple-element.18), channel_id=1, source_target_pairs={{0,1},{1,0},{2,3},{3,2},{4,5},{5,4},{6,7},{7,6},{8,9},{9,8},{10,11... | collective-permute-start | bytes 393224 | tf_op jit(solution)/shard_map/ppermute | solution.py:324
  23.9 0.1 add_add_fusion
  24.0 0.1 add.108
  24.0 0.1 add.100
  24.2 0.3 select_reduce_fusion
  24.4 0.1 add.97
  24.5 0.1 add.98
  24.7 0.1 compare_select_fusion.mask_ref
  24.8 1.7 %stage.1 = (bf16[2,512,1024]{2,1,0:T(8,128)(2,1)S(1)}, bf16[2,512,256]{2,1,0:T(8,128)(2,1)S(1)}) custom-call(bf16[2,512,1024]{2,1,0:T(8,128)(2,1)} %prefix_hbm.1, bf16[2,512,1024]{2,1,0:T(8,128)(2,1)} %bitcast.20), custom_call_target="tpu_custom_call" | custom-call | bytes 5242880 | tf_op jit(solution)/shard_map/stage/pallas_call | solution.py:74
  26.5 11.5 %all-to-all-done.query_ref = bf16[64,32,128]{2,1,0:T(8,128)(2,1)S(1)} async-done(((bf16[64,32,128]{2,1,0:T(8,128)(2,1)}), bf16[64,32,128]{2,1,0:T(8,128)(2,1)S(1)}, u32[]{:S(2)}, u32[]{:S(2)}) %all-to-all-start) | async-done | bytes 524320 | tf_op jit(solution)/shard_map/all_to_all | solution.py:23
  38.0 3.7 %attend.1 = bf16[2176,128]{1,0:T(8,128)(2,1)S(1)} custom-call(bf16[64,32,128]{2,1,0:T(8,128)(2,1)S(1)} %all-to-all-done.query_ref, bf16[2,512,1024]{2,1,0:T(8,128)(2,1)S(1)} %get-tuple-element.10.keys_ref, bf16[2,512,256]{2,1,0:T(8,128)(2,1)S(1)} %get-tuple-element.11.early_ref, bf16[2,512,1024]{2,1,0:T(8,128)(2,1)} %prefix_hbm.1, ...), custom_call_target="tpu_custom_call" | custom-call | flops 1073741824 | bytes 5242880 | tf_op jit(solution)/shard_map/attend/pallas_call | solution.py:174
  41.7 0.0 collective-permute-done.other_ref
  41.7 24.5 %all_to_all.20 = bf16[64,17,2,128]{3,2,1,0:T(2,128)(2,1)S(1)} all-to-all(bf16[64,17,2,128]{3,2,1,0:T(2,128)(2,1)S(1)} %bitcast.17), channel_id=1, replica_groups=mesh['req'=8,'y'=8,'zh'=4,'zl'=2] {'y','zh','zl'}, dimensions={0} | all-to-all | bytes 1114112 | tf_op jit(solution)/shard_map/all_to_all | solution.py:23
  66.3 0.4 merge.1
  66.7 10.4 %all_to_all.21 = bf16[16,32,128]{2,1,0:T(8,128)(2,1)S(1)} all-to-all(bf16[16,32,128]{2,1,0:T(8,128)(2,1)S(1)} %get-tuple-element.15), channel_id=1, replica_groups=mesh['req'=8,'y'=8,'zh'=4,'zl'=2] {'req','zl'}, dimensions={0} | all-to-all | bytes 262144 | tf_op jit(solution)/shard_map/all_to_all | solution.py:23
  77.1 0.9 project.1
  78.0 5.9 %all-to-all-start.3 = ((bf16[64,16,128]{2,1,0:T(8,128)(2,1)}), bf16[64,16,128]{2,1,0:T(8,128)(2,1)S(1)}, u32[]{:S(2)}, u32[]{:S(2)}) async-start(bf16[64,16,128]{2,1,0:T(8,128)(2,1)} %project.1), calls=%async_computation.3 | async-start | bytes 524288 | tf_op jit(solution)/shard_map/all_to_all | solution.py:23
  83.9 0.6 copy.12
  84.5 14.6 %all-to-all-done.3 = bf16[64,16,128]{2,1,0:T(8,128)(2,1)S(1)} async-done(((bf16[64,16,128]{2,1,0:T(8,128)(2,1)}), bf16[64,16,128]{2,1,0:T(8,128)(2,1)S(1)}, u32[]{:S(2)}, u32[]{:S(2)}) %all-to-all-start.3) | async-done | bytes 262176 | tf_op jit(solution)/shard_map/all_to_all | solution.py:23
  99.2 0.7 convert_reduce_fusion
  (12 shorter events, 0.1 us)
Async XLA Ops:
  0.6 0.7 copy-start
  1.3 22.5 %copy-start.2 = (s32[8]{0:T(128)S(1)}, s32[8]{0:T(128)}, u32[]{:S(2)}) copy-start(s32[8]{0:T(128)} %param.9) | copy-start | bytes 100
  1.3 22.8 %copy-start.1 = (s32[8,256]{1,0:T(8,128)S(1)}, s32[8,256]{1,0:T(8,128)}, u32[]{:S(2)}) copy-start(s32[8,256]{1,0:T(8,128)} %param.10) | copy-start | bytes 24580
  2.2 35.9 %all-to-all-start = ((bf16[64,32,128]{2,1,0:T(8,128)(2,1)}), bf16[64,32,128]{2,1,0:T(8,128)(2,1)S(1)}, u32[]{:S(2)}, u32[]{:S(2)}) async-start(bf16[64,32,128]{2,1,0:T(8,128)(2,1)} %spread.1), calls=%async_computation | async-start | bytes 1048576 | tf_op jit(solution)/shard_map/all_to_all | solution.py:23
  20.4 21.3 %collective-permute-start = (bf16[128,512]{1,0:T(8,128)(2,1)}, bf16[128,512]{1,0:T(8,128)(2,1)S(1)}, u32[]{:S(2)}, u32[]{:S(2)}) collective-permute-start(bf16[128,512]{1,0:T(8,128)(2,1)} %get-tuple-element.18), channel_id=1, source_target_pairs={{0,1},{1,0},{2,3},{3,2},{4,5},{5,4},{6,7},{7,6},{8,9},{9,8},{10,11... | collective-permute-start | bytes 393224 | tf_op jit(solution)/shard_map/ppermute | solution.py:324
  78.0 21.1 %all-to-all-start.3 = ((bf16[64,16,128]{2,1,0:T(8,128)(2,1)}), bf16[64,16,128]{2,1,0:T(8,128)(2,1)S(1)}, u32[]{:S(2)}, u32[]{:S(2)}) async-start(bf16[64,16,128]{2,1,0:T(8,128)(2,1)} %project.1), calls=%async_computation.3 | async-start | bytes 524288 | tf_op jit(solution)/shard_map/all_to_all | solution.py:23

commit v6 on v5

--- a/solution.py
+++ b/solution.py
@@ -197,8 +197,9 @@
     )(gathered, in_vmem(keys), in_vmem(early), in_hbm(prefix_cache), in_hbm(suffix_cache), mask)
 
 
-def merge_kernel(received_ref, merged_ref, copies_ref):
-    rows = merged_ref.shape[0]
+def merge_kernel(received_ref, attended_ref, copies_ref):
+    steps, requests, _ = attended_ref.shape
+    rows = steps * requests
     lines = rows + SPARE
     holders = received_ref.shape[0] // lines
     tiles = received_ref.shape[0] // HD
@@ -236,18 +237,23 @@
     low = (weights - high.astype(jnp.float32)).astype(jnp.bfloat16)
     sums = jnp.dot(jnp.concatenate([high, low], 0), received_ref[...], preferred_element_type=jnp.float32)
     merged = sums[:rows] + sums[rows:]
-    merged_ref[...] = merged
+    by_step = [
+        merged[request * steps + step : request * steps + step + 1]
+        for step in range(steps)
+        for request in range(requests)
+    ]
+    attended_ref[...] = jnp.concatenate(by_step, 0).reshape(steps, requests, HD)
     rounded = merged.astype(jnp.bfloat16)
     for copy in range(copies_ref.shape[0]):
         copies_ref[copy] = rounded
 
 
-def merge(received, rows, copies):
+def merge(received, steps, requests, copies):
     return pl.pallas_call(
         merge_kernel,
         out_shape=[
-            jax.ShapeDtypeStruct((rows, HD), jnp.float32),
-            jax.ShapeDtypeStruct((copies, rows, HD), jnp.bfloat16),
+            jax.ShapeDtypeStruct((steps, requests, HD), jnp.float32),
+            jax.ShapeDtypeStruct((copies, steps * requests, HD), jnp.bfloat16),
         ],
         name="merge",
         compiler_params=pltpu.CompilerParams(vmem_limit_bytes=16 * MEGA),
@@ -329,13 +335,11 @@
     mask = suffix_mask(page_table, suffix_lengths, holder, slot_count, page_length, step_count)
     shares = attend(gathered, *stage(prefix_cache, suffix_cache), prefix_cache, suffix_cache, mask)
     shares, own_half, other_half = lax.optimization_barrier((shares, own_half, other_half))
-    rows = step_count * local_requests
     members = lax.axis_size("req")
     shape = shares.shape
     shares = exchange(shares.reshape(holders, -1, SPARE, HD), PRE).reshape(shape)
-    merged, copies = merge(shares, rows, 2 * members)
-    attended = jnp.transpose(merged.reshape(local_requests, step_count, HD), (1, 0, 2))
-    lines = exchange(copies, ("req", "zl")).reshape((members, 2) + merged.shape)
+    attended, copies = merge(shares, step_count, local_requests, 2 * members)
+    lines = exchange(copies, ("req", "zl")).reshape((members, 2) + copies.shape[1:])
     pieces = exchange(project(lines, own_half, other_half, holders, side.reshape(1)), PRE)
     sums = jnp.sum(pieces.astype(jnp.float32).reshape((-1, 2) + pieces.shape[1:]), axis=0)
     projected = jnp.transpose(sums.reshape(-1, step_count, HD), (1, 0, 2)).reshape(step_count, -1)

time: 100 us -> 99.9 us (level)
  blocking collectives: 34.9 us -> 55.8 us
  waiting for transfers between devices: 26.2 us -> 11.5 us
  starting transfers between devices: 25.9 us -> 20.1 us
    all_to_all x2 -> x3, blocking collectives: 34.9 us -> 55.8 us  [exchange(): return lax.all_to_all(blocks, axis, 0, 0, tiled=True)]
    all_to_all x2 -> x1, waiting for transfers between devices: 26.2 us -> 11.5 us  [exchange(): return lax.all_to_all(blocks, axis, 0, 0, tiled=True)]
    all_to_all x2 -> x1, starting transfers between devices: 22.5 us -> 16.6 us  [exchange(): return lax.all_to_all(blocks, axis, 0, 0, tiled=True)]
  transfers between devices with their start and end apart: 3 -> 2, of which waited for: 2 -> 1; matrix products, arithmetic and copies ran while one was open for 3% -> 2% of each run, Pallas kernels for 5% -> 5%
where the time goes in v6:
time: 99.9 us; the launch traced here: 99.5 us
  blocking collectives  55.8 us (56%)
  starting transfers between devices  20.1 us (20%)
  waiting for transfers between devices  11.5 us (12%)
  Pallas kernels  7.5 us (8%)
  local copies, waits for them, and re-layouts  2.73 us (3%)
  other arithmetic  1.09 us (1%)
    all_to_all x3, blocking collectives, exchange(): return lax.all_to_all(blocks, axis, 0, 0, tiled=True)  55.8 us
    all_to_all x1, starting transfers between devices, exchange(): return lax.all_to_all(blocks, axis, 0, 0, tiled=True)  16.6 us
    all_to_all x1, waiting for transfers between devices, exchange(): return lax.all_to_all(blocks, axis, 0, 0, tiled=True)  11.5 us
    pallas_call x1, Pallas kernels, attend(): pl.pallas_call(attend_kernel, in_specs=[pl.BlockSpec(memory_space=pltpu.V...  3.69 us
    ppermute x1, starting transfers between devices, body(): other_half = lax.ppermute(other_half, 'zl', [(0, 1), (1, 0)])  3.47 us
  transfers between devices with their start and end apart: 2, of which 1 were waited for; matrix products, arithmetic and copies ran while one was open for 2% of the time, Pallas kernels for 5%

profile of v6, /device:TPU:2, one launch (start us, length us, event | category | flops | bytes accessed | tf_op | source)
XLA Modules:
  0.0 99.5 jit_solution(14516205799837580577)
XLA Ops:
  0.6 0.0 copy-start
  0.6 0.7 copy-done
  1.3 0.8 spread.1
  2.2 16.6 %all-to-all-start = ((bf16[64,32,128]{2,1,0:T(8,128)(2,1)}), bf16[64,32,128]{2,1,0:T(8,128)(2,1)S(1)}, u32[]{:S(2)}, u32[]{:S(2)}) async-start(bf16[64,32,128]{2,1,0:T(8,128)(2,1)} %spread.1), calls=%async_computation | async-start | bytes 1048576 | tf_op jit(solution)/shard_map/all_to_all | solution.py:23
  18.8 1.6 %constant_dynamic-slice_fusion = (bf16[128,512]{1,0:T(8,128)(2,1)}, bf16[128,512]{1,0:T(8,128)(2,1)S(1)}) fusion(bf16[128,1024]{1,0:T(8,128)(2,1)} %param.11, s32[]{:T(128)S(6)} %select_n.27, s32[]{:T(128)S(6)} %select_n.26), kind=kLoop, calls=%fused_computation.7 | loop fusion | bytes 524296 | tf_op jit(solution)/shard_map/dynamic_slice | solution.py:329
  20.4 3.5 %collective-permute-start = (bf16[128,512]{1,0:T(8,128)(2,1)}, bf16[128,512]{1,0:T(8,128)(2,1)S(1)}, u32[]{:S(2)}, u32[]{:S(2)}) collective-permute-start(bf16[128,512]{1,0:T(8,128)(2,1)} %get-tuple-element.18), channel_id=1, source_target_pairs={{0,1},{1,0},{2,3},{3,2},{4,5},{5,4},{6,7},{7,6},{8,9},{9,8},{10,11... | collective-permute-start | bytes 393224 | tf_op jit(solution)/shard_map/ppermute | solution.py:330
  23.9 0.0 copy-done.2
  23.9 0.1 add_add_fusion
  24.0 0.1 add.108
  24.0 0.1 add.100
  24.1 0.3 select_reduce_fusion
  24.4 0.1 add.97
  24.5 0.1 add.98
  24.7 0.1 compare_select_fusion.mask_ref
  24.8 1.7 %stage.1 = (bf16[2,512,1024]{2,1,0:T(8,128)(2,1)S(1)}, bf16[2,512,256]{2,1,0:T(8,128)(2,1)S(1)}) custom-call(bf16[2,512,1024]{2,1,0:T(8,128)(2,1)} %prefix_hbm.1, bf16[2,512,1024]{2,1,0:T(8,128)(2,1)} %bitcast.15), custom_call_target="tpu_custom_call" | custom-call | bytes 5242880 | tf_op jit(solution)/shard_map/stage/pallas_call | solution.py:74
  26.5 11.5 %all-to-all-done.query_ref = bf16[64,32,128]{2,1,0:T(8,128)(2,1)S(1)} async-done(((bf16[64,32,128]{2,1,0:T(8,128)(2,1)}), bf16[64,32,128]{2,1,0:T(8,128)(2,1)S(1)}, u32[]{:S(2)}, u32[]{:S(2)}) %all-to-all-start) | async-done | bytes 524320 | tf_op jit(solution)/shard_map/all_to_all | solution.py:23
  38.0 3.7 %attend.1 = bf16[2176,128]{1,0:T(8,128)(2,1)S(1)} custom-call(bf16[64,32,128]{2,1,0:T(8,128)(2,1)S(1)} %all-to-all-done.query_ref, bf16[2,512,1024]{2,1,0:T(8,128)(2,1)S(1)} %get-tuple-element.10.keys_ref, bf16[2,512,256]{2,1,0:T(8,128)(2,1)S(1)} %get-tuple-element.11.early_ref, bf16[2,512,1024]{2,1,0:T(8,128)(2,1)} %prefix_hbm.1, ...), custom_call_target="tpu_custom_call" | custom-call | flops 1073741824 | bytes 5242880 | tf_op jit(solution)/shard_map/attend/pallas_call | solution.py:174
  41.7 0.0 collective-permute-done.other_ref
  41.7 24.5 %all_to_all.20 = bf16[64,17,2,128]{3,2,1,0:T(2,128)(2,1)S(1)} all-to-all(bf16[64,17,2,128]{3,2,1,0:T(2,128)(2,1)S(1)} %bitcast.13), channel_id=1, replica_groups=mesh['req'=8,'y'=8,'zh'=4,'zl'=2] {'y','zh','zl'}, dimensions={0} | all-to-all | bytes 1114112 | tf_op jit(solution)/shard_map/all_to_all | solution.py:23
  66.3 1.1 %merge.1 = (f32[4,8,128]{2,1,0:T(8,128)}, bf16[16,32,128]{2,1,0:T(8,128)(2,1)S(1)}) custom-call(bf16[2176,128]{1,0:T(8,128)(2,1)S(1)} %bitcast.12), custom_call_target="tpu_custom_call" | custom-call | tf_op jit(solution)/shard_map/merge/pallas_call | solution.py:252
  67.3 10.3 %all_to_all.21 = bf16[16,32,128]{2,1,0:T(8,128)(2,1)S(1)} all-to-all(bf16[16,32,128]{2,1,0:T(8,128)(2,1)S(1)} %get-tuple-element.15), channel_id=1, replica_groups=mesh['req'=8,'y'=8,'zh'=4,'zl'=2] {'req','zl'}, dimensions={0} | all-to-all | bytes 262144 | tf_op jit(solution)/shard_map/all_to_all | solution.py:23
  77.7 0.2 project.1
  77.9 21.0 %all_to_all.22 = bf16[64,16,128]{2,1,0:T(8,128)(2,1)S(1)} all-to-all(bf16[64,16,128]{2,1,0:T(8,128)(2,1)S(1)} %project.1), channel_id=1, replica_groups=mesh['req'=8,'y'=8,'zh'=4,'zl'=2] {'y','zh','zl'}, dimensions={0} | all-to-all | bytes 524288 | tf_op jit(solution)/shard_map/all_to_all | solution.py:23
  98.9 0.7 convert_reduce_fusion
  (10 shorter events, 0.1 us)
Async XLA Ops:
  0.6 0.7 copy-start
  1.3 22.5 %copy-start.2 = (s32[8]{0:T(128)S(1)}, s32[8]{0:T(128)}, u32[]{:S(2)}) copy-start(s32[8]{0:T(128)} %param.9) | copy-start | bytes 100
  1.3 22.8 %copy-start.1 = (s32[8,256]{1,0:T(8,128)S(1)}, s32[8,256]{1,0:T(8,128)}, u32[]{:S(2)}) copy-start(s32[8,256]{1,0:T(8,128)} %param.10) | copy-start | bytes 24580
  2.2 35.9 %all-to-all-start = ((bf16[64,32,128]{2,1,0:T(8,128)(2,1)}), bf16[64,32,128]{2,1,0:T(8,128)(2,1)S(1)}, u32[]{:S(2)}, u32[]{:S(2)}) async-start(bf16[64,32,128]{2,1,0:T(8,128)(2,1)} %spread.1), calls=%async_computation | async-start | bytes 1048576 | tf_op jit(solution)/shard_map/all_to_all | solution.py:23
  20.4 21.3 %collective-permute-start = (bf16[128,512]{1,0:T(8,128)(2,1)}, bf16[128,512]{1,0:T(8,128)(2,1)S(1)}, u32[]{:S(2)}, u32[]{:S(2)}) collective-permute-start(bf16[128,512]{1,0:T(8,128)(2,1)} %get-tuple-element.18), channel_id=1, source_target_pairs={{0,1},{1,0},{2,3},{3,2},{4,5},{5,4},{6,7},{7,6},{8,9},{9,8},{10,11... | collective-permute-start | bytes 393224 | tf_op jit(solution)/shard_map/ppermute | solution.py:330
